TPU v7x, 128 devices: a whole 4x4x4 slice. The times are simulated.
128 devices in a mesh: lon: 16 (over z, y_hi, core), lat: 8 (over x, y_lo).
Axes of the slice: x: 4, y: 4 (y_hi: 2, y_lo: 2; y = y_hi * 2 + y_lo), z: 4, core: 2. Of those that a mesh axis runs over, the one named last changes fastest.
Arguments:
- offset_input: bfloat16 [196, 64, 8192], P(None, 'lat', 'lon'), may hold values from -6 to 6
- current: bfloat16 [64, 64, 8192], P(None, 'lat', 'lon'), may hold values from -6 to 6
- source: bfloat16 [64, 64, 8192], P(None, 'lat', 'lon'), may hold values from -6 to 6
- first_weight: bfloat16 [9, 64, 196], replicated, may hold values from -0.125 to 0.125
- second_weight: bfloat16 [9, 64, 64], replicated, may hold values from -0.25 to 0.25
- mask_weight: bfloat16 [9, 144, 64], replicated, may hold values from -0.25 to 0.25
- deform_weight: bfloat16 [9, 64, 64], replicated, may hold values from -0.25 to 0.25
- merge_weight: bfloat16 [9, 64, 128], replicated, may hold values from -0.1875 to 0.1875
- residual_weight: bfloat16 [2, 2, 9, 64, 64], replicated, may hold values from -0.25 to 0.25
- footprint: int32 [64, 64, 9, 2], P('lat', 'lon'), may hold values from 0 to 4095, as said below
- tile_scale: float32 [64, 64, 9, 2], P('lat', 'lon'), may hold values from 0.5 to 2
- hats: bfloat16 [64, 64, 9, 2, 128, 128], P('lat', 'lon'), may hold values from -0.375 to 0.375
Outputs:
- propagated: bfloat16 [64, 64, 8192], P(None, 'lat', 'lon')
Inputs may be any that keep to these rules, and one draw needn't show every extreme that they name: `footprint`: each id is row * 64 + block of a source block. For the reader at row y and block j the row lies within 2 of y (clamped to the frame) and the block lies within r blocks of j around the longitude loop, where r = max(1, ceil(2 |2 y - 63| / 64)) is 2 at the first and last rows; both distances are reached in every draw.
All inputs are finite; a program needn't handle non-finite values.
Results may differ from a plain program's by a relative error of at most 0.015.
Values may be sent and summed in bfloat16 or wider, within the bound.
A program may use at most 128 MiB of HBM per device.

v0:
```python
import jax
import jax.numpy as jnp
from jax import lax
from jax.sharding import PartitionSpec as P

BLK = 128
FP = 2
RY = 2


def with_halo(cells, sides, width, closed):
    for axis, dim in sides:
        count = lax.axis_size(axis)
        ends = count if closed else count - 1
        head = lax.slice_in_dim(cells, 0, width, axis=dim)
        tail = lax.slice_in_dim(cells, cells.shape[dim] - width, cells.shape[dim], axis=dim)
        cells = jnp.concatenate(
            [
                lax.ppermute(tail, axis, [(i, (i + 1) % count) for i in range(ends)]),
                cells,
                lax.ppermute(head, axis, [((i + 1) % count, i) for i in range(ends)]),
            ],
            axis=dim,
        )
    return cells


def leaky_unit(values):
    return jnp.where(values > 0, values, 0.1 * values)


def conv_valid(padded, weight):
    height = padded.shape[1] - 2
    width = padded.shape[2] - 2
    accumulated = jnp.zeros((weight.shape[1], height, width), jnp.float32)
    for kernel_tap in range(9):
        row_shift = kernel_tap // 3
        col_shift = kernel_tap % 3
        window = padded[:, row_shift : row_shift + height, col_shift : col_shift + width]
        accumulated = accumulated + jnp.einsum(
            "oc,chw->ohw", weight[kernel_tap], window, preferred_element_type=jnp.float32
        )
    return accumulated


def extend(values, margin):
    wider = with_halo(values, (("lon", 2),), margin, True)
    return with_halo(wider, (("lat", 1),), margin, False)


def layer(values, weight):
    return conv_valid(extend(values, 1), weight)


def shards(
    offset_input,
    current,
    source,
    first_weight,
    second_weight,
    mask_weight,
    deform_weight,
    merge_weight,
    residual_weight,
    footprint,
    tile_scale,
    hats,
):
    channels = source.shape[0]
    tile_rows = source.shape[1]
    tile_cols = source.shape[2]
    row_blocks = tile_cols // BLK
    group_count = mask_weight.shape[1] // 9
    hidden_one = leaky_unit(layer(offset_input, first_weight)).astype(jnp.bfloat16)
    hidden_two = leaky_unit(layer(hidden_one, second_weight)).astype(jnp.bfloat16)
    modulation = jax.nn.sigmoid(layer(hidden_two, mask_weight))
    src_wide = with_halo(source, (("lon", 2),), row_blocks * BLK, True)
    src_window = with_halo(src_wide, (("lat", 1),), RY, False)
    window_rows = tile_rows + 2 * RY
    window_blocks = row_blocks + 2 * row_blocks
    blocks = src_window.reshape(channels, window_rows, window_blocks, BLK).transpose(1, 2, 0, 3)
    blocks = blocks.reshape(window_rows * window_blocks, channels, BLK)
    total_blocks = row_blocks * lax.axis_size("lon")
    src_rows = footprint // total_blocks
    src_cols = footprint % total_blocks
    local_rows = src_rows - lax.axis_index("lat") * tile_rows + RY
    local_cols = (src_cols - lax.axis_index("lon") * row_blocks + row_blocks) % total_blocks
    flat_index = (local_rows * window_blocks + local_cols).reshape(-1)
    picked = jnp.take(blocks, flat_index, axis=0).reshape(
        tile_rows, row_blocks, 9, FP, channels, BLK
    )
    products = jnp.einsum("hjkfcs,hjkfsd->hjkfcd", picked, hats, preferred_element_type=jnp.float32)
    sampled = jnp.sum(products * tile_scale[:, :, :, :, None, None], axis=3)
    sampled = sampled.transpose(2, 3, 0, 1, 4).reshape(9, channels, tile_rows, tile_cols)
    modulated = modulation.reshape(9, group_count, 1, tile_rows, tile_cols) * sampled.reshape(
        9, group_count, channels // group_count, tile_rows, tile_cols
    )
    modulated = modulated.reshape(9, channels, tile_rows, tile_cols).astype(jnp.bfloat16)
    aligned = jnp.einsum(
        "koc,kchw->ohw", deform_weight, modulated, preferred_element_type=jnp.float32
    ).astype(jnp.bfloat16)
    joined = jnp.concatenate([current, aligned], axis=0)
    trunk = leaky_unit(layer(joined, merge_weight)).astype(jnp.bfloat16)
    for block_index in range(residual_weight.shape[0]):
        inner = jax.nn.relu(layer(trunk, residual_weight[block_index, 0])).astype(jnp.bfloat16)
        trunk = (trunk.astype(jnp.float32) + layer(inner, residual_weight[block_index, 1])).astype(
            jnp.bfloat16
        )
    return (trunk.astype(jnp.float32) + aligned.astype(jnp.float32)).astype(jnp.bfloat16)


def solution(mesh):
    in_specs = (
        P(None, "lat", "lon"),
        P(None, "lat", "lon"),
        P(None, "lat", "lon"),
        P(),
        P(),
        P(),
        P(),
        P(),
        P(),
        P("lat", "lon", None, None),
        P("lat", "lon", None, None),
        P("lat", "lon", None, None, None, None),
    )
    out_specs = P(None, "lat", "lon")
    return jax.shard_map(shards, mesh=mesh, in_specs=in_specs, out_specs=out_specs, check_vma=False)
```

profile of v0, /device:TPU:0, one launch (start us, length us, event | category | flops | bytes accessed | tf_op | source)
XLA Modules:
  0.0 302.4 jit_solution(5306492130172080837)
XLA Ops:
  2.0 6.2 %collective-permute-start.13 = (bf16[64,8,512]{2,0,1:T(8,128)(2,1)}, bf16[64,8,512]{2,0,1:T(8,128)(2,1)}, u32[]{:S(2)}, u32[]{:S(2)}) collective-permute-start(bf16[64,8,512]{2,0,1:T(8,128)(2,1)} %copy.59), channel_id=1, source_target_pairs={{8,0},{16,8},{24,16},{32,24},{40,32},{48,40},{56,48},{64,56},{72,6... | collective-permute-start | bytes 1572872 | tf_op jit(solution)/shard_map/ppermute | solution.py:21
  11.2 5.4 %collective-permute-start.1 = (bf16[196,8,1]{2,0,1:T(8,128)(2,1)}, bf16[196,8,1]{2,0,1:T(8,128)(2,1)S(1)}, u32[]{:S(2)}, u32[]{:S(2)}) collective-permute-start(bf16[196,8,1]{2,0,1:T(8,128)(2,1)} %get-tuple-element.12), channel_id=1, source_target_pairs={{8,0},{16,8},{24,16},{32,24},{40,32},{48,40},{56,48},{64,56},{72,6... | collective-permute-start | bytes 9416 | tf_op jit(solution)/shard_map/ppermute | solution.py:21
  24.6 5.9 %collective-permute-done = bf16[196,8,1]{2,0,1:T(8,128)(2,1)S(1)} collective-permute-done((bf16[196,8,1]{2,0,1:T(8,128)(2,1)}, bf16[196,8,1]{2,0,1:T(8,128)(2,1)S(1)}, u32[]{:S(2)}, u32[]{:S(2)}) %collective-permute-start) | collective-permute-done | bytes 3168 | tf_op jit(solution)/shard_map/ppermute | solution.py:19
  37.9 4.4 %collective-permute-done.3 = bf16[196,1,514]{2,0,1:T(8,128)(2,1)S(1)} collective-permute-done((bf16[196,1,514]{2,0,1:T(8,128)(2,1)S(1)}, bf16[196,1,514]{2,0,1:T(8,128)(2,1)S(1)}, u32[]{:S(2)}, u32[]{:S(2)}) %collective-permute-start.3) | collective-permute-done | bytes 201520 | tf_op jit(solution)/shard_map/ppermute | solution.py:21
  50.6 5.3 %collective-permute-start.5 = (bf16[64,8,1]{2,0,1:T(8,128)(2,1)S(1)}, bf16[64,8,1]{2,0,1:T(8,128)(2,1)S(1)}, u32[]{:S(2)}, u32[]{:S(2)}) collective-permute-start(bf16[64,8,1]{2,0,1:T(8,128)(2,1)S(1)} %get-tuple-element.56), channel_id=1, source_target_pairs={{8,0},{16,8},{24,16},{32,24},{40,32},{48,40},{56,48},{64,56},{72,6... | collective-permute-start | bytes 3080 | tf_op jit(solution)/shard_map/ppermute | solution.py:21
  58.7 4.4 %collective-permute-start.6 = (bf16[64,1,514]{2,0,1:T(8,128)(2,1)S(1)}, bf16[64,1,514]{2,0,1:T(8,128)(2,1)S(1)}, u32[]{:S(2)}, u32[]{:S(2)}) collective-permute-start(bf16[64,1,514]{2,0,1:T(8,128)(2,1)S(1)} %get-tuple-element.43), channel_id=1, source_target_pairs={{0,1},{1,2},{2,3},{3,4},{4,5},{5,6},{6,7},{8,9},{9,10},{10,11},{11... | collective-permute-start | bytes 197384 | tf_op jit(solution)/shard_map/ppermute | solution.py:19
  73.1 5.3 %collective-permute-start.9 = (bf16[64,8,1]{2,0,1:T(8,128)(2,1)S(1)}, bf16[64,8,1]{2,0,1:T(8,128)(2,1)S(1)}, u32[]{:S(2)}, u32[]{:S(2)}) collective-permute-start(bf16[64,8,1]{2,0,1:T(8,128)(2,1)S(1)} %get-tuple-element.54), channel_id=1, source_target_pairs={{8,0},{16,8},{24,16},{32,24},{40,32},{48,40},{56,48},{64,56},{72,6... | collective-permute-start | bytes 3080 | tf_op jit(solution)/shard_map/ppermute | solution.py:21
  108.3 6.1 %collective-permute-done.14 = bf16[64,2,1536]{2,0,1:T(8,128)(2,1)S(1)} collective-permute-done((bf16[64,2,1536]{2,0,1:T(8,128)(2,1)S(1)}, bf16[64,2,1536]{2,0,1:T(8,128)(2,1)S(1)}, u32[]{:S(2)}, u32[]{:S(2)}) %collective-permute-start.14) | collective-permute-done | bytes 393248 | tf_op jit(solution)/shard_map/ppermute | solution.py:19
  120.7 18.1 %gather_fusion = bf16[576,64,128]{2,1,0:T(8,128)(2,1)} fusion(bf16[144,64,128]{2,1,0:T(8,128)(2,1)S(1)} %bitcast.413, s32[1024]{0:T(1024)S(1)} %copy-done.13), kind=kCustom, calls=%fused_computation | custom fusion | bytes 18876672 | tf_op jit(solution)/shard_map/jit(_take)/gather | solution.py:89
  138.8 16.4 %multiply_reduce_fusion = f32[8,4,9,64,128]{4,3,2,1,0:T(8,128)} fusion(f32[8,4,9,2]{3,2,1,0:T(8,128)S(1)} %copy-done.4, bf16[8,4,9,2,128,128]{5,4,3,2,1,0:T(8,128)(2,1)} %param.23, bf16[8,4,9,2,64,128]{5,4,3,2,1,0:T(8,128)(2,1)} %bitcast.414, pred[8,4,9,2]{3,2,1,0:T(8,128)(4,1)S(1)} %copy-done.8), kind=kOutput, calls=%fused_computation.1 | convolution fusion | flops 1219756032 | bytes 37751616 | tf_op jit(solution)/shard_map/hjkfcs,hjkfsd->hjkfcd/dot_general | solution.py:92
  155.3 4.9 %mul.45 = f32[9,16,4,8,512]{4,3,2,1,0:T(8,128)} broadcast(f32[9,16,8,512]{3,2,1,0:T(8,128)S(1)} %copy-done.1), dimensions={0,1,3,4} | broadcast | bytes 11796480 | tf_op jit(solution)/shard_map/mul | solution.py:95
  160.2 15.2 %fusion = bf16[9,64,8,512]{3,2,1,0:T(8,128)(2,1)} fusion(f32[9,64,8,512]{3,2,1,0:T(8,128)} %bitcast.415, f32[9,64,8,4,128]{4,1,0,3,2:T(8,128)} %bitcast.416), kind=kLoop, calls=%fused_computation.3 | loop fusion | flops 4718592 | bytes 23592960 | tf_op jit(solution)/shard_map/convert_element_type | solution.py:98
  175.4 5.2 %fusion.126 = bf16[64,8,512]{2,0,1:T(8,128)(2,1)S(1)} fusion(bf16[9,64,8,512]{3,2,1,0:T(8,128)(2,1)} %fusion, bf16[9,64,64]{2,1,0:T(8,128)(2,1)S(1)} %copy-done), kind=kOutput, calls=%fused_computation.118 | convolution fusion | flops 302252032 | bytes 5316608 | tf_op jit(solution)/shard_map/koc,kchw->ohw/dot_general | solution.py:99
  180.9 5.4 %collective-permute-start.17 = (bf16[128,8,1]{2,0,1:T(8,128)(2,1)S(1)}, bf16[128,8,1]{2,0,1:T(8,128)(2,1)S(1)}, u32[]{:S(2)}, u32[]{:S(2)}) collective-permute-start(bf16[128,8,1]{2,0,1:T(8,128)(2,1)S(1)} %get-tuple-element.20), channel_id=1, source_target_pairs={{8,0},{16,8},{24,16},{32,24},{40,32},{48,40},{56,48},{64,56},{72,6... | collective-permute-start | bytes 6152 | tf_op jit(solution)/shard_map/ppermute | solution.py:21
  186.6 5.3 %collective-permute-done.16 = bf16[128,8,1]{2,0,1:T(8,128)(2,1)S(1)} collective-permute-done((bf16[128,8,1]{2,0,1:T(8,128)(2,1)S(1)}, bf16[128,8,1]{2,0,1:T(8,128)(2,1)S(1)}, u32[]{:S(2)}, u32[]{:S(2)}) %collective-permute-start.16) | collective-permute-done | bytes 2080 | tf_op jit(solution)/shard_map/ppermute | solution.py:19
  192.1 4.6 %collective-permute-start.18 = (bf16[128,1,514]{2,0,1:T(8,128)(2,1)S(1)}, bf16[128,1,514]{2,0,1:T(8,128)(2,1)S(1)}, u32[]{:S(2)}, u32[]{:S(2)}) collective-permute-start(bf16[128,1,514]{2,0,1:T(8,128)(2,1)S(1)} %get-tuple-element.15), channel_id=1, source_target_pairs={{0,1},{1,2},{2,3},{3,4},{4,5},{5,6},{6,7},{8,9},{9,10},{10,11},{11... | collective-permute-start | bytes 394760 | tf_op jit(solution)/shard_map/ppermute | solution.py:19
  199.5 4.8 %collective-permute-done.19 = bf16[128,1,514]{2,0,1:T(8,128)(2,1)S(1)} collective-permute-done((bf16[128,1,514]{2,0,1:T(8,128)(2,1)S(1)}, bf16[128,1,514]{2,0,1:T(8,128)(2,1)S(1)}, u32[]{:S(2)}, u32[]{:S(2)}) %collective-permute-start.19) | collective-permute-done | bytes 131616 | tf_op jit(solution)/shard_map/ppermute | solution.py:21
  210.9 5.3 %collective-permute-start.21 = (bf16[64,8,1]{2,0,1:T(8,128)(2,1)S(1)}, bf16[64,8,1]{2,0,1:T(8,128)(2,1)S(1)}, u32[]{:S(2)}, u32[]{:S(2)}) collective-permute-start(bf16[64,8,1]{2,0,1:T(8,128)(2,1)S(1)} %get-tuple-element.52), channel_id=1, source_target_pairs={{8,0},{16,8},{24,16},{32,24},{40,32},{48,40},{56,48},{64,56},{72,6... | collective-permute-start | bytes 3080 | tf_op jit(solution)/shard_map/ppermute | solution.py:21
  219.0 4.5 %collective-permute-start.22 = (bf16[64,1,514]{2,0,1:T(8,128)(2,1)S(1)}, bf16[64,1,514]{2,0,1:T(8,128)(2,1)S(1)}, u32[]{:S(2)}, u32[]{:S(2)}) collective-permute-start(bf16[64,1,514]{2,0,1:T(8,128)(2,1)S(1)} %get-tuple-element.35), channel_id=1, source_target_pairs={{0,1},{1,2},{2,3},{3,4},{4,5},{5,6},{6,7},{8,9},{9,10},{10,11},{11... | collective-permute-start | bytes 197384 | tf_op jit(solution)/shard_map/ppermute | solution.py:19
  233.3 5.3 %collective-permute-start.25 = (bf16[64,8,1]{2,0,1:T(8,128)(2,1)S(1)}, bf16[64,8,1]{2,0,1:T(8,128)(2,1)S(1)}, u32[]{:S(2)}, u32[]{:S(2)}) collective-permute-start(bf16[64,8,1]{2,0,1:T(8,128)(2,1)S(1)} %get-tuple-element.50), channel_id=1, source_target_pairs={{8,0},{16,8},{24,16},{32,24},{40,32},{48,40},{56,48},{64,56},{72,6... | collective-permute-start | bytes 3080 | tf_op jit(solution)/shard_map/ppermute | solution.py:21
  242.4 5.0 %collective-permute-start.26 = (bf16[64,1,514]{2,0,1:T(8,128)(2,1)S(1)}, bf16[64,1,514]{2,0,1:T(8,128)(2,1)S(1)}, u32[]{:S(2)}, u32[]{:S(2)}) collective-permute-start(bf16[64,1,514]{2,0,1:T(8,128)(2,1)S(1)} %get-tuple-element.31), channel_id=1, source_target_pairs={{0,1},{1,2},{2,3},{3,4},{4,5},{5,6},{6,7},{8,9},{9,10},{10,11},{11... | collective-permute-start | bytes 197384 | tf_op jit(solution)/shard_map/ppermute | solution.py:19
  257.2 5.3 %collective-permute-start.29 = (bf16[64,8,1]{2,0,1:T(8,128)(2,1)S(1)}, bf16[64,8,1]{2,0,1:T(8,128)(2,1)S(1)}, u32[]{:S(2)}, u32[]{:S(2)}) collective-permute-start(bf16[64,8,1]{2,0,1:T(8,128)(2,1)S(1)} %get-tuple-element.48), channel_id=1, source_target_pairs={{8,0},{16,8},{24,16},{32,24},{40,32},{48,40},{56,48},{64,56},{72,6... | collective-permute-start | bytes 3080 | tf_op jit(solution)/shard_map/ppermute | solution.py:21
  270.2 4.7 %collective-permute-done.31 = bf16[64,1,514]{2,0,1:T(8,128)(2,1)S(1)} collective-permute-done((bf16[64,1,514]{2,0,1:T(8,128)(2,1)S(1)}, bf16[64,1,514]{2,0,1:T(8,128)(2,1)S(1)}, u32[]{:S(2)}, u32[]{:S(2)}) %collective-permute-start.31) | collective-permute-done | bytes 65824 | tf_op jit(solution)/shard_map/ppermute | solution.py:21
  278.2 5.3 %collective-permute-start.33 = (bf16[64,8,1]{2,0,1:T(8,128)(2,1)S(1)}, bf16[64,8,1]{2,0,1:T(8,128)(2,1)S(1)}, u32[]{:S(2)}, u32[]{:S(2)}) collective-permute-start(bf16[64,8,1]{2,0,1:T(8,128)(2,1)S(1)} %get-tuple-element.46), channel_id=1, source_target_pairs={{8,0},{16,8},{24,16},{32,24},{40,32},{48,40},{56,48},{64,56},{72,6... | collective-permute-start | bytes 3080 | tf_op jit(solution)/shard_map/ppermute | solution.py:21
  (196 shorter events, 142.4 us)
Async XLA Ops:
  2.0 94.4 %collective-permute-start.13 = (bf16[64,8,512]{2,0,1:T(8,128)(2,1)}, bf16[64,8,512]{2,0,1:T(8,128)(2,1)}, u32[]{:S(2)}, u32[]{:S(2)}) collective-permute-start(bf16[64,8,512]{2,0,1:T(8,128)(2,1)} %copy.59), channel_id=1, source_target_pairs={{8,0},{16,8},{24,16},{32,24},{40,32},{48,40},{56,48},{64,56},{72,6... | collective-permute-start | bytes 1572872 | tf_op jit(solution)/shard_map/ppermute | solution.py:21
  8.2 86.9 %collective-permute-start.12 = (bf16[64,8,512]{2,0,1:T(8,128)(2,1)}, bf16[64,8,512]{2,0,1:T(8,128)(2,1)}, u32[]{:S(2)}, u32[]{:S(2)}) collective-permute-start(bf16[64,8,512]{2,0,1:T(8,128)(2,1)} %copy.59), channel_id=1, source_target_pairs={{0,8},{8,16},{16,24},{24,32},{32,40},{40,48},{48,56},{56,64},{64,7... | collective-permute-start | bytes 1572872 | tf_op jit(solution)/shard_map/ppermute | solution.py:19
  11.2 19.3 %collective-permute-start = (bf16[196,8,1]{2,0,1:T(8,128)(2,1)}, bf16[196,8,1]{2,0,1:T(8,128)(2,1)S(1)}, u32[]{:S(2)}, u32[]{:S(2)}) collective-permute-start(bf16[196,8,1]{2,0,1:T(8,128)(2,1)} %get-tuple-element.11), channel_id=1, source_target_pairs={{0,8},{8,16},{16,24},{24,32},{32,40},{40,48},{48,56},{56,64},{64,7... | collective-permute-start | bytes 9416 | tf_op jit(solution)/shard_map/ppermute | solution.py:19
  11.2 19.3 %collective-permute-start.1 = (bf16[196,8,1]{2,0,1:T(8,128)(2,1)}, bf16[196,8,1]{2,0,1:T(8,128)(2,1)S(1)}, u32[]{:S(2)}, u32[]{:S(2)}) collective-permute-start(bf16[196,8,1]{2,0,1:T(8,128)(2,1)} %get-tuple-element.12), channel_id=1, source_target_pairs={{8,0},{16,8},{24,16},{32,24},{40,32},{48,40},{56,48},{64,56},{72,6... | collective-permute-start | bytes 9416 | tf_op jit(solution)/shard_map/ppermute | solution.py:21
  34.1 8.2 %collective-permute-start.3 = (bf16[196,1,514]{2,0,1:T(8,128)(2,1)S(1)}, bf16[196,1,514]{2,0,1:T(8,128)(2,1)S(1)}, u32[]{:S(2)}, u32[]{:S(2)}) collective-permute-start(bf16[196,1,514]{2,0,1:T(8,128)(2,1)S(1)} %get-tuple-element.10), channel_id=1, source_target_pairs={{1,0},{2,1},{3,2},{4,3},{5,4},{6,5},{7,6},{9,8},{10,9},{11,10},{12... | collective-permute-start | bytes 604472 | tf_op jit(solution)/shard_map/ppermute | solution.py:21
  50.5 8.1 %collective-permute-start.4 = (bf16[64,8,1]{2,0,1:T(8,128)(2,1)S(1)}, bf16[64,8,1]{2,0,1:T(8,128)(2,1)S(1)}, u32[]{:S(2)}, u32[]{:S(2)}) collective-permute-start(bf16[64,8,1]{2,0,1:T(8,128)(2,1)S(1)} %get-tuple-element.55), channel_id=1, source_target_pairs={{0,8},{8,16},{16,24},{24,32},{32,40},{40,48},{48,56},{56,64},{64,7... | collective-permute-start | bytes 3080 | tf_op jit(solution)/shard_map/ppermute | solution.py:19
  50.6 8.0 %collective-permute-start.5 = (bf16[64,8,1]{2,0,1:T(8,128)(2,1)S(1)}, bf16[64,8,1]{2,0,1:T(8,128)(2,1)S(1)}, u32[]{:S(2)}, u32[]{:S(2)}) collective-permute-start(bf16[64,8,1]{2,0,1:T(8,128)(2,1)S(1)} %get-tuple-element.56), channel_id=1, source_target_pairs={{8,0},{16,8},{24,16},{32,24},{40,32},{48,40},{56,48},{64,56},{72,6... | collective-permute-start | bytes 3080 | tf_op jit(solution)/shard_map/ppermute | solution.py:21
  72.8 8.8 %collective-permute-start.8 = (bf16[64,8,1]{2,0,1:T(8,128)(2,1)S(1)}, bf16[64,8,1]{2,0,1:T(8,128)(2,1)S(1)}, u32[]{:S(2)}, u32[]{:S(2)}) collective-permute-start(bf16[64,8,1]{2,0,1:T(8,128)(2,1)S(1)} %get-tuple-element.53), channel_id=1, source_target_pairs={{0,8},{8,16},{16,24},{24,32},{32,40},{40,48},{48,56},{56,64},{64,7... | collective-permute-start | bytes 3080 | tf_op jit(solution)/shard_map/ppermute | solution.py:19
  73.1 8.5 %collective-permute-start.9 = (bf16[64,8,1]{2,0,1:T(8,128)(2,1)S(1)}, bf16[64,8,1]{2,0,1:T(8,128)(2,1)S(1)}, u32[]{:S(2)}, u32[]{:S(2)}) collective-permute-start(bf16[64,8,1]{2,0,1:T(8,128)(2,1)S(1)} %get-tuple-element.54), channel_id=1, source_target_pairs={{8,0},{16,8},{24,16},{32,24},{40,32},{48,40},{56,48},{64,56},{72,6... | collective-permute-start | bytes 3080 | tf_op jit(solution)/shard_map/ppermute | solution.py:21
  97.6 16.8 %collective-permute-start.14 = (bf16[64,2,1536]{2,0,1:T(8,128)(2,1)S(1)}, bf16[64,2,1536]{2,0,1:T(8,128)(2,1)S(1)}, u32[]{:S(2)}, u32[]{:S(2)}) collective-permute-start(bf16[64,2,1536]{2,0,1:T(8,128)(2,1)S(1)} %get-tuple-element.17), channel_id=1, source_target_pairs={{0,1},{1,2},{2,3},{3,4},{4,5},{5,6},{6,7},{8,9},{9,10},{10,11},{11... | collective-permute-start | bytes 1179656 | tf_op jit(solution)/shard_map/ppermute | solution.py:19
  101.5 12.8 %collective-permute-start.15 = (bf16[64,2,1536]{2,0,1:T(8,128)(2,1)S(1)}, bf16[64,2,1536]{2,0,1:T(8,128)(2,1)S(1)}, u32[]{:S(2)}, u32[]{:S(2)}) collective-permute-start(bf16[64,2,1536]{2,0,1:T(8,128)(2,1)S(1)} %get-tuple-element.18), channel_id=1, source_target_pairs={{1,0},{2,1},{3,2},{4,3},{5,4},{6,5},{7,6},{9,8},{10,9},{11,10},{12... | collective-permute-start | bytes 1179656 | tf_op jit(solution)/shard_map/ppermute | solution.py:21
  180.8 11.1 %collective-permute-start.16 = (bf16[128,8,1]{2,0,1:T(8,128)(2,1)S(1)}, bf16[128,8,1]{2,0,1:T(8,128)(2,1)S(1)}, u32[]{:S(2)}, u32[]{:S(2)}) collective-permute-start(bf16[128,8,1]{2,0,1:T(8,128)(2,1)S(1)} %get-tuple-element.19), channel_id=1, source_target_pairs={{0,8},{8,16},{16,24},{24,32},{32,40},{40,48},{48,56},{56,64},{64,7... | collective-permute-start | bytes 6152 | tf_op jit(solution)/shard_map/ppermute | solution.py:19
  180.9 11.0 %collective-permute-start.17 = (bf16[128,8,1]{2,0,1:T(8,128)(2,1)S(1)}, bf16[128,8,1]{2,0,1:T(8,128)(2,1)S(1)}, u32[]{:S(2)}, u32[]{:S(2)}) collective-permute-start(bf16[128,8,1]{2,0,1:T(8,128)(2,1)S(1)} %get-tuple-element.20), channel_id=1, source_target_pairs={{8,0},{16,8},{24,16},{32,24},{40,32},{48,40},{56,48},{64,56},{72,6... | collective-permute-start | bytes 6152 | tf_op jit(solution)/shard_map/ppermute | solution.py:21
  192.1 7.5 %collective-permute-start.18 = (bf16[128,1,514]{2,0,1:T(8,128)(2,1)S(1)}, bf16[128,1,514]{2,0,1:T(8,128)(2,1)S(1)}, u32[]{:S(2)}, u32[]{:S(2)}) collective-permute-start(bf16[128,1,514]{2,0,1:T(8,128)(2,1)S(1)} %get-tuple-element.15), channel_id=1, source_target_pairs={{0,1},{1,2},{2,3},{3,4},{4,5},{5,6},{6,7},{8,9},{9,10},{10,11},{11... | collective-permute-start | bytes 394760 | tf_op jit(solution)/shard_map/ppermute | solution.py:19
  196.7 7.6 %collective-permute-start.19 = (bf16[128,1,514]{2,0,1:T(8,128)(2,1)S(1)}, bf16[128,1,514]{2,0,1:T(8,128)(2,1)S(1)}, u32[]{:S(2)}, u32[]{:S(2)}) collective-permute-start(bf16[128,1,514]{2,0,1:T(8,128)(2,1)S(1)} %get-tuple-element.16), channel_id=1, source_target_pairs={{1,0},{2,1},{3,2},{4,3},{5,4},{6,5},{7,6},{9,8},{10,9},{11,10},{12... | collective-permute-start | bytes 394760 | tf_op jit(solution)/shard_map/ppermute | solution.py:21
  210.8 8.1 %collective-permute-start.20 = (bf16[64,8,1]{2,0,1:T(8,128)(2,1)S(1)}, bf16[64,8,1]{2,0,1:T(8,128)(2,1)S(1)}, u32[]{:S(2)}, u32[]{:S(2)}) collective-permute-start(bf16[64,8,1]{2,0,1:T(8,128)(2,1)S(1)} %get-tuple-element.51), channel_id=1, source_target_pairs={{0,8},{8,16},{16,24},{24,32},{32,40},{40,48},{48,56},{56,64},{64,7... | collective-permute-start | bytes 3080 | tf_op jit(solution)/shard_map/ppermute | solution.py:19
  210.9 8.0 %collective-permute-start.21 = (bf16[64,8,1]{2,0,1:T(8,128)(2,1)S(1)}, bf16[64,8,1]{2,0,1:T(8,128)(2,1)S(1)}, u32[]{:S(2)}, u32[]{:S(2)}) collective-permute-start(bf16[64,8,1]{2,0,1:T(8,128)(2,1)S(1)} %get-tuple-element.52), channel_id=1, source_target_pairs={{8,0},{16,8},{24,16},{32,24},{40,32},{48,40},{56,48},{64,56},{72,6... | collective-permute-start | bytes 3080 | tf_op jit(solution)/shard_map/ppermute | solution.py:21
  233.2 9.1 %collective-permute-start.24 = (bf16[64,8,1]{2,0,1:T(8,128)(2,1)S(1)}, bf16[64,8,1]{2,0,1:T(8,128)(2,1)S(1)}, u32[]{:S(2)}, u32[]{:S(2)}) collective-permute-start(bf16[64,8,1]{2,0,1:T(8,128)(2,1)S(1)} %get-tuple-element.49), channel_id=1, source_target_pairs={{0,8},{8,16},{16,24},{24,32},{32,40},{40,48},{48,56},{56,64},{64,7... | collective-permute-start | bytes 3080 | tf_op jit(solution)/shard_map/ppermute | solution.py:19
  233.3 9.0 %collective-permute-start.25 = (bf16[64,8,1]{2,0,1:T(8,128)(2,1)S(1)}, bf16[64,8,1]{2,0,1:T(8,128)(2,1)S(1)}, u32[]{:S(2)}, u32[]{:S(2)}) collective-permute-start(bf16[64,8,1]{2,0,1:T(8,128)(2,1)S(1)} %get-tuple-element.50), channel_id=1, source_target_pairs={{8,0},{16,8},{24,16},{32,24},{40,32},{48,40},{56,48},{64,56},{72,6... | collective-permute-start | bytes 3080 | tf_op jit(solution)/shard_map/ppermute | solution.py:21
  242.4 7.1 %collective-permute-start.26 = (bf16[64,1,514]{2,0,1:T(8,128)(2,1)S(1)}, bf16[64,1,514]{2,0,1:T(8,128)(2,1)S(1)}, u32[]{:S(2)}, u32[]{:S(2)}) collective-permute-start(bf16[64,1,514]{2,0,1:T(8,128)(2,1)S(1)} %get-tuple-element.31), channel_id=1, source_target_pairs={{0,1},{1,2},{2,3},{3,4},{4,5},{5,6},{6,7},{8,9},{9,10},{10,11},{11... | collective-permute-start | bytes 197384 | tf_op jit(solution)/shard_map/ppermute | solution.py:19
  257.1 8.1 %collective-permute-start.28 = (bf16[64,8,1]{2,0,1:T(8,128)(2,1)S(1)}, bf16[64,8,1]{2,0,1:T(8,128)(2,1)S(1)}, u32[]{:S(2)}, u32[]{:S(2)}) collective-permute-start(bf16[64,8,1]{2,0,1:T(8,128)(2,1)S(1)} %get-tuple-element.47), channel_id=1, source_target_pairs={{0,8},{8,16},{16,24},{24,32},{32,40},{40,48},{48,56},{56,64},{64,7... | collective-permute-start | bytes 3080 | tf_op jit(solution)/shard_map/ppermute | solution.py:19
  257.2 8.0 %collective-permute-start.29 = (bf16[64,8,1]{2,0,1:T(8,128)(2,1)S(1)}, bf16[64,8,1]{2,0,1:T(8,128)(2,1)S(1)}, u32[]{:S(2)}, u32[]{:S(2)}) collective-permute-start(bf16[64,8,1]{2,0,1:T(8,128)(2,1)S(1)} %get-tuple-element.48), channel_id=1, source_target_pairs={{8,0},{16,8},{24,16},{32,24},{40,32},{48,40},{56,48},{64,56},{72,6... | collective-permute-start | bytes 3080 | tf_op jit(solution)/shard_map/ppermute | solution.py:21
  278.1 9.0 %collective-permute-start.32 = (bf16[64,8,1]{2,0,1:T(8,128)(2,1)S(1)}, bf16[64,8,1]{2,0,1:T(8,128)(2,1)S(1)}, u32[]{:S(2)}, u32[]{:S(2)}) collective-permute-start(bf16[64,8,1]{2,0,1:T(8,128)(2,1)S(1)} %get-tuple-element.45), channel_id=1, source_target_pairs={{0,8},{8,16},{16,24},{24,32},{32,40},{40,48},{48,56},{56,64},{64,7... | collective-permute-start | bytes 3080 | tf_op jit(solution)/shard_map/ppermute | solution.py:19
  278.2 8.9 %collective-permute-start.33 = (bf16[64,8,1]{2,0,1:T(8,128)(2,1)S(1)}, bf16[64,8,1]{2,0,1:T(8,128)(2,1)S(1)}, u32[]{:S(2)}, u32[]{:S(2)}) collective-permute-start(bf16[64,8,1]{2,0,1:T(8,128)(2,1)S(1)} %get-tuple-element.46), channel_id=1, source_target_pairs={{8,0},{16,8},{24,16},{32,24},{40,32},{48,40},{56,48},{64,56},{72,6... | collective-permute-start | bytes 3080 | tf_op jit(solution)/shard_map/ppermute | solution.py:21
  (26 other events, 380.9 us)
where the time goes:
time: 307 us; the launch traced here: 302 us
  starting transfers between devices  98.4 us (32%)
  waiting for transfers between devices  71.6 us (23%)
  matrix products  59.7 us (19%)
  local copies, waits for them, and re-layouts  44.7 us (15%)
  other arithmetic  26.7 us (9%)
    ppermute x18, starting transfers between devices, with_halo(): lax.ppermute(head, axis, [((i + 1) % count, i) for i in range(ends)])  61.3 us
    dot_general x72, matrix products, conv_valid(): jnp.einsum('oc,chw->ohw', weight[kernel_tap], window, preferred_element_t...  38 us
    ppermute x18, waiting for transfers between devices, with_halo(): lax.ppermute(tail, axis, [(i, (i + 1) % count) for i in range(ends)])  37.1 us
    ppermute x18, starting transfers between devices, with_halo(): lax.ppermute(tail, axis, [(i, (i + 1) % count) for i in range(ends)])  37.1 us
    ppermute x18, waiting for transfers between devices, with_halo(): lax.ppermute(head, axis, [((i + 1) % count, i) for i in range(ends)])  34.5 us
    gather x1, local copies, waits for them, and re-layouts, shards(): jnp.take(blocks, flat_index, axis=0)  18.1 us
    dot_general x1, matrix products, shards(): jnp.einsum('hjkfcs,hjkfsd->hjkfcd', picked, hats, preferred_element_type=...  16.4 us
    convert_element_type x1, other arithmetic, shards(): modulated.reshape(9, channels, tile_rows, tile_cols).astype(jnp.bfloat16)  15.2 us
  transfers between devices with their start and end apart: 36, of which 25 were waited for; matrix products, arithmetic and copies ran while one was open for 13% of the time, Pallas kernels for 0%

commit v1 on v0

v1 whole, which is shorter than its diff:
```python
import functools

import jax
import jax.numpy as jnp
from jax import lax
from jax.experimental import pallas as pl
from jax.experimental.pallas import tpu as pltpu
from jax.sharding import PartitionSpec as P

BF = jnp.bfloat16
F32 = jnp.float32
MESH = pl.DeviceIdType.MESH

BLK = 128
ROWS = 8
COLS = 512
WIDE = 640
CIN = 196
CPAD = 256
NB = COLS // BLK
WIN_ROWS = ROWS + 4
WIN_COLS = NB + 4
TAPS = 9
K2 = 18

LEFT, RIGHT, UP, DOWN, UL, UR, DL, DR = range(8)
OPP = (RIGHT, LEFT, DOWN, UP, DR, DL, UR, UL)
S_OFF, S_SRC, S_SRC_LO, S_SRC_HI, S_CURM, S_CUR, S_PART, S_H1, S_ALM, S_AL, S_T0, S_T1 = range(12)


def leaky(v):
    return jnp.where(v > 0, v, 0.1 * v)


def kernel(
    n_lon, n_lat,
    off_hbm, cur_hbm, src_hbm, w1_ref, w2_ref, wm_ref, wd_ref, wg_ref, wr_ref,
    idx_ref, scale_ref, hats_hbm, out_ref,
    raw_off, raw_src, raw_cur, stage, hats, win, sampled, modulated,
    v0, h1, h2, joined, t0, i0, t1, i1,
    w1, w2, wm, wd, wg, wr,
    pack_off, got_off, pack_cur, got_cur, pack_al, got_al,
    part_out, part_in, part_own,
    load_sem, hat_sem, send_sem, recv_sem,
):
    lon = lax.axis_index("lon")
    lat = lax.axis_index("lat")
    left = lax.rem(lon + n_lon - 1, n_lon)
    right = lax.rem(lon + 1, n_lon)
    has_up = lat > 0
    has_down = lat < n_lat - 1
    nb = {
        LEFT: (None, (left, lat)), RIGHT: (None, (right, lat)),
        UP: (has_up, (lon, lat - 1)), DOWN: (has_down, (lon, lat + 1)),
        UL: (has_up, (left, lat - 1)), UR: (has_up, (right, lat - 1)),
        DL: (has_down, (left, lat + 1)), DR: (has_down, (right, lat + 1)),
    }

    def guarded(cond, fn):
        if cond is None:
            fn()
        else:
            pl.when(cond)(fn)

    def copy(kind, direction, src, dst):
        return pltpu.make_async_remote_copy(
            src_ref=src, dst_ref=dst,
            send_sem=send_sem.at[kind, direction],
            recv_sem=recv_sem.at[kind, OPP[direction]],
            device_id=nb[direction][1], device_id_type=MESH,
        )

    def send(kind, direction, src, dst):
        guarded(nb[direction][0], lambda: copy(kind, direction, src, dst).start())

    def wait_send(kind, direction, src):
        def go():
            pltpu.make_async_remote_copy(
                src_ref=src, dst_ref=src, send_sem=send_sem.at[kind, direction],
                recv_sem=recv_sem.at[kind, direction],
                device_id=nb[direction][1], device_id_type=MESH,
            ).wait_send()
        guarded(nb[direction][0], go)

    def wait_recv(kind, direction, dst):
        def go():
            pltpu.make_async_remote_copy(
                src_ref=dst, dst_ref=dst, send_sem=send_sem.at[kind, direction],
                recv_sem=recv_sem.at[kind, direction],
                device_id=nb[direction][1], device_id_type=MESH,
            ).wait_recv()
        guarded(nb[direction][0], go)

    load_off = pltpu.make_async_copy(off_hbm, raw_off, load_sem.at[0])
    load_src = pltpu.make_async_copy(src_hbm, raw_src, load_sem.at[1])
    load_cur = pltpu.make_async_copy(cur_hbm, raw_cur, load_sem.at[2])
    load_off.start()
    load_src.start()
    load_cur.start()

    def hat_load(y):
        return pltpu.make_async_copy(hats_hbm.at[y], hats.at[y], hat_sem.at[y])

    for y in range(ROWS):
        hat_load(y).start()

    def zero_rows(buf, lo, hi):
        buf[lo:hi] = jnp.zeros((hi - lo,) + buf.shape[1:], buf.dtype)

    for buf, m in ((h1, 2), (joined, 1), (t0, 2), (t1, 2)):
        zero_rows(buf, 0, m)
        zero_rows(buf, ROWS + m, ROWS + 2 * m)
    zero_rows(v0, 0, 1)
    zero_rows(v0, ROWS + 1, ROWS + 2)
    part_in[...] = jnp.zeros(part_in.shape, BF)
    got_cur[...] = jnp.zeros(got_cur.shape, BF)
    got_al[...] = jnp.zeros(got_al.shape, BF)
    pack_off[...] = jnp.zeros(pack_off.shape, BF)
    for i in range(1, ROWS + 1):
        v0[i, 192:CPAD, :] = jnp.zeros((CPAD - 192, WIDE), BF)

    barrier = pltpu.get_barrier_semaphore()
    for d in range(8):
        guarded(nb[d][0], lambda d=d: pl.semaphore_signal(
            barrier, inc=1, device_id=nb[d][1], device_id_type=MESH))
    both = has_up & has_down
    pl.when(both)(lambda: pl.semaphore_wait(barrier, 8))
    pl.when(jnp.logical_not(both))(lambda: pl.semaphore_wait(barrier, 5))

    lane = lax.broadcasted_iota(jnp.int32, (1, BLK), 1)

    def pack_tiles(tiles, side):
        total = None
        for y, tile in enumerate(tiles):
            shift = 8 * y if side == 0 else 8 * y + 8
            moved = pltpu.roll(tile, shift, 1) if shift else tile
            here = (lane >= 8 * y) & (lane < 8 * y + 8)
            total = jnp.where(here, moved, 0.0 if total is None else total)
        return total

    def unpack(from_right, from_left, y):
        a = pltpu.roll(from_right, (128 - 8 * y) % 128, 1) if y else from_right
        b = pltpu.roll(from_left, 120 - 8 * y, 1)
        return jnp.where(lane < 8, a, jnp.where(lane >= 120, b, 0.0))

    load_off.wait()
    for j in range(NB):
        stage[j] = raw_off[:, j * BLK:(j + 1) * BLK].astype(F32)

    def staged(channels, y, j):
        return stage[j, pl.ds(y, channels, stride=ROWS), :]

    pack_off[0, 0:CIN, :] = pack_tiles(
        [staged(CIN, y, 0) for y in range(ROWS)], 0).astype(BF)
    pack_off[1, 0:CIN, :] = pack_tiles(
        [staged(CIN, y, NB - 1) for y in range(ROWS)], 1).astype(BF)
    send(S_OFF, LEFT, pack_off.at[0], got_off.at[0])
    send(S_OFF, RIGHT, pack_off.at[1], got_off.at[1])

    def v0_row(y, _):
        for j in range(NB):
            v0[y + 1, 0:CIN, j * BLK:(j + 1) * BLK] = staged(CIN, y, j).astype(BF)
        return 0

    lax.fori_loop(0, ROWS, v0_row, 0)

    load_src.wait()
    for j in range(NB):
        stage[j, 0:512, :] = raw_src[:, j * BLK:(j + 1) * BLK].astype(F32)

    def win_row(y, _):
        for k in range(4):
            for j in range(NB):
                win[y + 2, j + 2, k * 16:(k + 1) * 16, :] = stage[
                    j, pl.ds(k * ROWS + y, 16, stride=4 * ROWS), :].astype(BF)
        return 0

    lax.fori_loop(0, ROWS, win_row, 0)
    w_lat_up, w_lat_dn = win.at[2:4, 2:6], win.at[8:10, 2:6]
    send(S_SRC, UP, w_lat_up, win.at[10:12, 2:6])
    send(S_SRC, DOWN, w_lat_dn, win.at[0:2, 2:6])
    w_left, w_right = win.at[2:10, 2:4], win.at[2:10, 4:6]
    send(S_SRC, LEFT, w_left, win.at[2:10, 6:8])
    send(S_SRC, RIGHT, w_right, win.at[2:10, 0:2])

    load_cur.wait()
    for j in range(NB):
        stage[j, 512:1024, :] = raw_cur[:, j * BLK:(j + 1) * BLK].astype(F32)

    def cur_staged(y, j):
        return stage[j, pl.ds(512 + y, 64, stride=ROWS), :]

    def cur_row(y, _):
        for j in range(NB):
            joined[y + 1, 0:64, j * BLK:(j + 1) * BLK] = cur_staged(y, j).astype(BF)
        return 0

    lax.fori_loop(0, ROWS, cur_row, 0)
    pack_cur[0] = pack_tiles([cur_staged(y, 0) for y in range(ROWS)], 0).astype(BF)
    pack_cur[1] = pack_tiles([cur_staged(y, NB - 1) for y in range(ROWS)], 1).astype(BF)

    w1[...] = jnp.zeros(w1.shape, BF)
    for a in range(3):
        for b in range(3):
            w1[b * 64:(b + 1) * 64, a * CPAD:a * CPAD + CIN] = w1_ref[3 * a + b]
            wg[b * 64:(b + 1) * 64, a * 128:(a + 1) * 128] = wg_ref[3 * a + b]
    for b in range(3):
        w2[b * 64:(b + 1) * 64, :] = jnp.concatenate([w2_ref[3 * a + b] for a in range(3)], axis=1)
        for r in range(4):
            wr[r, b * 64:(b + 1) * 64, :] = jnp.concatenate(
                [wr_ref[r, 3 * a + b] for a in range(3)], axis=1)
    wm[...] = jnp.concatenate([wm_ref[t] for t in range(TAPS)], axis=1)
    row_id = lax.broadcasted_iota(jnp.int32, (64, 64), 0)
    col_id = lax.broadcasted_iota(jnp.int32, (64, 64), 1)
    perm = (row_id == (col_id % 16) * 4 + col_id // 16).astype(BF)
    wd[...] = jnp.concatenate(
        [jnp.dot(wd_ref[t], perm, preferred_element_type=F32).astype(BF) for t in range(TAPS)], axis=1)

    def spread(p):
        n = p.shape[1]
        return pltpu.roll(p[0:64], 1, 1) + p[64:128] + pltpu.roll(p[128:192], n - 1, 1)

    def conv_row(src, i, weight):
        x = src[pl.ds(i, 3)].reshape(3 * src.shape[1], WIDE)
        return spread(jnp.dot(weight, x, preferred_element_type=F32))

    wait_recv(S_OFF, RIGHT, got_off.at[0])
    wait_recv(S_OFF, LEFT, got_off.at[1])
    for y in range(ROWS):
        v0[y + 1, 0:CIN, COLS:WIDE] = unpack(
            got_off[0, 0:CIN, :].astype(F32), got_off[1, 0:CIN, :].astype(F32), y).astype(BF)
    part_out[0] = spread(jnp.dot(w1[:, 2 * CPAD:], v0[1], preferred_element_type=F32)).astype(BF)
    part_out[1] = spread(jnp.dot(w1[:, :CPAD], v0[ROWS], preferred_element_type=F32)).astype(BF)
    send(S_PART, UP, part_out.at[0], part_in.at[1])
    send(S_PART, DOWN, part_out.at[1], part_in.at[0])

    def h1_row(y, _):
        h1[y + 2] = leaky(conv_row(v0, y, w1[...])).astype(BF)
        return 0

    part_own[0] = conv_row(v0, 0, w1[...])
    part_own[1] = conv_row(v0, ROWS - 1, w1[...])
    lax.fori_loop(1, ROWS - 1, h1_row, 0)

    wait_recv(S_SRC, UP, win.at[0:2, 2:6])
    wait_recv(S_SRC, DOWN, win.at[10:12, 2:6])

    def relay(kind, rows):
        send(kind, LEFT, win.at[rows, 2:4], win.at[rows, 6:8])
        send(kind, RIGHT, win.at[rows, 4:6], win.at[rows, 0:2])

    pl.when(has_up)(lambda: relay(S_SRC_LO, slice(0, 2)))
    pl.when(has_down)(lambda: relay(S_SRC_HI, slice(10, 12)))

    wait_recv(S_PART, UP, part_in.at[0])
    wait_recv(S_PART, DOWN, part_in.at[1])
    h1[2] = leaky(part_own[0] + part_in[0].astype(F32)).astype(BF)
    h1[ROWS + 1] = leaky(part_own[1] + part_in[1].astype(F32)).astype(BF)

    def edges_out(kind, buf, count, m):
        send(kind, UP, buf.at[m:m + count], buf.at[ROWS + m:ROWS + m + count])
        send(kind, DOWN, buf.at[ROWS + m - count:ROWS + m], buf.at[m - count:m])

    def edges_in(kind, buf, count, m):
        wait_recv(kind, UP, buf.at[m - count:m])
        wait_recv(kind, DOWN, buf.at[ROWS + m:ROWS + m + count])

    def edges_sent(kind, buf, count, m):
        wait_send(kind, UP, buf.at[m:m + count])
        wait_send(kind, DOWN, buf.at[ROWS + m - count:ROWS + m])

    edges_out(S_H1, h1, 2, 2)

    for side, dirs in ((0, (LEFT, UL, DL)), (1, (RIGHT, UR, DR))):
        for d in dirs:
            send(S_CURM, d, pack_cur.at[side], got_cur.at[OPP[d]])
    send(S_CUR, UP, joined.at[1, 0:64, 0:COLS], joined.at[ROWS + 1, 0:64, 0:COLS])
    send(S_CUR, DOWN, joined.at[ROWS, 0:64, 0:COLS], joined.at[0, 0:64, 0:COLS])

    def in_frame(y):
        g = lat * ROWS + y
        return (g >= 0) & (g < n_lat * ROWS)

    def h2_row(y, _):
        v = leaky(conv_row(h1, y + 1, w2[...]))
        v = jnp.where(in_frame(y), v, 0.0)
        h2[y + 1, 0:64] = pltpu.roll(v, 1, 1).astype(BF)
        h2[y + 1, 64:128] = v.astype(BF)
        h2[y + 1, 128:192] = pltpu.roll(v, WIDE - 1, 1).astype(BF)
        return 0

    lax.fori_loop(1, ROWS - 1, h2_row, 0)

    wait_recv(S_SRC, RIGHT, win.at[2:10, 6:8])
    wait_recv(S_SRC, LEFT, win.at[2:10, 0:2])

    def relayed(kind, rows):
        wait_recv(kind, RIGHT, win.at[rows, 6:8])
        wait_recv(kind, LEFT, win.at[rows, 0:2])

    pl.when(has_up)(lambda: relayed(S_SRC_LO, slice(0, 2)))
    pl.when(has_down)(lambda: relayed(S_SRC_HI, slice(10, 12)))

    for y in range(ROWS):
        hat_load(y).wait()

    def sample_row(y, _):
        for j in range(NB):
            for t in range(TAPS):
                at = (y * NB + j) * K2 + 2 * t
                parts = []
                for f in range(2):
                    ix = idx_ref[at + f]
                    blk = win[lax.shift_right_logical(ix, 3), lax.bitwise_and(ix, 7)]
                    parts.append((blk.astype(F32) * scale_ref[at + f]).astype(BF))
                tile = hats[y, (j * K2 + 2 * t) * BLK:(j * K2 + 2 * t + 2) * BLK, :]
                sampled[y, t * 64:(t + 1) * 64, j * BLK:(j + 1) * BLK] = jnp.dot(
                    jnp.concatenate(parts, axis=1), tile, preferred_element_type=F32)
        return 0

    lax.fori_loop(0, ROWS, sample_row, 0)

    def aligned_row(y, _):
        x = h2[pl.ds(y, 3)].reshape(576, WIDE)[:, 0:COLS]
        logits = jnp.dot(wm[...], x, preferred_element_type=F32)
        mod = 1.0 / (1.0 + jnp.exp(-logits))
        for t in range(TAPS):
            m = mod[t * 16:(t + 1) * 16]
            for k in range(4):
                lo = t * 64 + k * 16
                modulated[lo:lo + 16, :] = (m * sampled[y, lo:lo + 16, :]).astype(BF)
        joined[y + 1, 64:128, 0:COLS] = jnp.dot(
            wd[...], modulated[...], preferred_element_type=F32).astype(BF)
        return 0

    lax.fori_loop(2, ROWS - 2, aligned_row, 0)

    def edge4(fn):
        return lambda i, c: fn(i + (i // 2) * (ROWS - 4), c)

    def ring4(fn):
        return lambda i, c: fn(i - 1 + (i // 2) * (ROWS - 2), c)

    edges_in(S_H1, h1, 2, 2)
    lax.fori_loop(0, 4, ring4(h2_row), 0)
    lax.fori_loop(0, 4, edge4(aligned_row), 0)

    send(S_AL, UP, joined.at[1, 64:128, 0:COLS], joined.at[ROWS + 1, 64:128, 0:COLS])
    send(S_AL, DOWN, joined.at[ROWS, 64:128, 0:COLS], joined.at[0, 64:128, 0:COLS])
    pack_al[0] = pack_tiles(
        [joined[y + 1, 64:128, 0:BLK].astype(F32) for y in range(ROWS)], 0).astype(BF)
    pack_al[1] = pack_tiles(
        [joined[y + 1, 64:128, COLS - BLK:COLS].astype(F32) for y in range(ROWS)], 1).astype(BF)
    for side, dirs in ((0, (LEFT, UL, DL)), (1, (RIGHT, UR, DR))):
        for d in dirs:
            send(S_ALM, d, pack_al.at[side], got_al.at[OPP[d]])

    def margins(kind, got, lo):
        for d in range(8):
            if d not in (UP, DOWN):
                wait_recv(kind, d, got.at[d])

        def put(i, from_right, from_left, y):
            joined[i, lo:lo + 64, COLS:WIDE] = unpack(
                got[from_right].astype(F32), got[from_left].astype(F32), y).astype(BF)

        for y in range(ROWS):
            put(y + 1, RIGHT, LEFT, y)
        put(0, UR, UL, ROWS - 1)
        put(ROWS + 1, DR, DL, 0)

    margins(S_CURM, got_cur, 0)
    margins(S_ALM, got_al, 64)

    def t0_row(y, _):
        t0[y + 2] = leaky(conv_row(joined, y, wg[...])).astype(BF)
        return 0

    def inner_row(dst, src, r):
        def go(y, _):
            v = jnp.maximum(conv_row(src, y + 1, wr[r]), 0.0)
            dst[y + 1] = jnp.where(in_frame(y), v, 0.0).astype(BF)
            return 0
        return go

    def t1_row(y, _):
        t1[y + 2] = (t0[y + 2].astype(F32) + conv_row(i0, y, wr[1])).astype(BF)
        return 0

    def final_row(y, _):
        trunk = (t1[y + 2].astype(F32) + conv_row(i1, y, wr[3])).astype(BF)
        trunk = trunk[:, 0:COLS].astype(F32)
        total = trunk + joined[y + 1, 64:128, 0:COLS].astype(F32)
        for j in range(NB):
            stage[j, pl.ds(y, 64, stride=ROWS), :] = total[:, j * BLK:(j + 1) * BLK]
        return 0

    lax.fori_loop(1, ROWS - 1, t0_row, 0)
    wait_recv(S_CUR, UP, joined.at[0, 0:64, 0:COLS])
    wait_recv(S_CUR, DOWN, joined.at[ROWS + 1, 0:64, 0:COLS])
    wait_recv(S_AL, UP, joined.at[0, 64:128, 0:COLS])
    wait_recv(S_AL, DOWN, joined.at[ROWS + 1, 64:128, 0:COLS])
    t0_row(0, 0)
    t0_row(ROWS - 1, 0)
    edges_out(S_T0, t0, 2, 2)
    inner0 = inner_row(i0, t0, 0)
    inner1 = inner_row(i1, t1, 2)
    lax.fori_loop(1, ROWS - 1, inner0, 0)
    lax.fori_loop(2, ROWS - 2, t1_row, 0)
    edges_in(S_T0, t0, 2, 2)
    lax.fori_loop(0, 4, ring4(inner0), 0)
    lax.fori_loop(0, 4, edge4(t1_row), 0)
    edges_out(S_T1, t1, 2, 2)
    lax.fori_loop(1, ROWS - 1, inner1, 0)
    lax.fori_loop(2, ROWS - 2, final_row, 0)
    edges_in(S_T1, t1, 2, 2)
    lax.fori_loop(0, 4, ring4(inner1), 0)
    lax.fori_loop(0, 4, edge4(final_row), 0)
    for j in range(NB):
        out_ref[:, j * BLK:(j + 1) * BLK] = stage[j, 0:512, :].astype(BF)

    wait_send(S_OFF, LEFT, pack_off.at[0])
    wait_send(S_OFF, RIGHT, pack_off.at[1])
    wait_send(S_SRC, UP, w_lat_up)
    wait_send(S_SRC, DOWN, w_lat_dn)
    wait_send(S_SRC, LEFT, w_left)
    wait_send(S_SRC, RIGHT, w_right)

    def relay_sent(kind, rows):
        wait_send(kind, LEFT, win.at[rows, 2:4])
        wait_send(kind, RIGHT, win.at[rows, 4:6])

    pl.when(has_up)(lambda: relay_sent(S_SRC_LO, slice(0, 2)))
    pl.when(has_down)(lambda: relay_sent(S_SRC_HI, slice(10, 12)))
    wait_send(S_PART, UP, part_out.at[0])
    wait_send(S_PART, DOWN, part_out.at[1])
    for side, dirs in ((0, (LEFT, UL, DL)), (1, (RIGHT, UR, DR))):
        for d in dirs:
            wait_send(S_CURM, d, pack_cur.at[side])
            wait_send(S_ALM, d, pack_al.at[side])
    wait_send(S_CUR, UP, joined.at[1, 0:64, 0:COLS])
    wait_send(S_CUR, DOWN, joined.at[ROWS, 0:64, 0:COLS])
    wait_send(S_AL, UP, joined.at[1, 64:128, 0:COLS])
    wait_send(S_AL, DOWN, joined.at[ROWS, 64:128, 0:COLS])
    edges_sent(S_H1, h1, 2, 2)
    edges_sent(S_T0, t0, 2, 2)
    edges_sent(S_T1, t1, 2, 2)


def shards(
    offset_input, current, source, first_weight, second_weight, mask_weight, deform_weight,
    merge_weight, residual_weight, footprint, tile_scale, hats,
):
    n_lon, n_lat = lax.axis_size("lon"), lax.axis_size("lat")
    total_blocks = NB * n_lon
    row = footprint // total_blocks - lax.axis_index("lat") * ROWS + 2
    col = (footprint % total_blocks - lax.axis_index("lon") * NB + 2) % total_blocks
    index = (row * WIN_COLS + col).reshape(-1)
    vmem = pl.BlockSpec(memory_space=pltpu.VMEM)
    smem = pl.BlockSpec(memory_space=pltpu.SMEM)
    hbm = pl.BlockSpec(memory_space=pl.ANY)
    V = pltpu.VMEM
    out = pl.pallas_call(
        functools.partial(kernel, n_lon, n_lat),
        out_shape=jax.ShapeDtypeStruct((64 * ROWS, COLS), BF),
        in_specs=[hbm, hbm, hbm] + [vmem] * 6 + [smem, smem, hbm],
        out_specs=vmem,
        scratch_shapes=[
            V((CIN * ROWS, COLS), BF), V((64 * ROWS, COLS), BF), V((64 * ROWS, COLS), BF),
            V((NB, CIN * ROWS, BLK), F32),
            V((ROWS, NB * K2 * BLK, BLK), BF),
            V((WIN_ROWS, WIN_COLS, 64, BLK), BF),
            V((ROWS, TAPS * 64, COLS), F32),
            V((TAPS * 64, COLS), BF),
            V((ROWS + 2, CPAD, WIDE), BF),
            V((ROWS + 4, 64, WIDE), BF),
            V((ROWS + 2, 192, WIDE), BF),
            V((ROWS + 2, 128, WIDE), BF),
            V((ROWS + 4, 64, WIDE), BF),
            V((ROWS + 2, 64, WIDE), BF),
            V((ROWS + 4, 64, WIDE), BF),
            V((ROWS + 2, 64, WIDE), BF),
            V((192, 3 * CPAD), BF), V((192, 192), BF), V((144, 576), BF), V((64, 576), BF),
            V((192, 384), BF), V((4, 192, 192), BF),
            V((2, 208, BLK), BF), V((2, 208, BLK), BF),
            V((2, 64, BLK), BF), V((8, 64, BLK), BF),
            V((2, 64, BLK), BF), V((8, 64, BLK), BF),
            V((2, 64, WIDE), BF), V((2, 64, WIDE), BF), V((2, 64, WIDE), F32),
            pltpu.SemaphoreType.DMA((3,)),
            pltpu.SemaphoreType.DMA((ROWS,)),
            pltpu.SemaphoreType.DMA((12, 8)),
            pltpu.SemaphoreType.DMA((12, 8)),
        ],
        compiler_params=pltpu.CompilerParams(
            collective_id=0, has_side_effects=True, vmem_limit_bytes=60 * 2**20),
    )(
        offset_input.reshape(CIN * ROWS, COLS),
        current.reshape(64 * ROWS, COLS),
        source.reshape(64 * ROWS, COLS),
        first_weight, second_weight, mask_weight, deform_weight, merge_weight,
        residual_weight.reshape(4, 9, 64, 64),
        index, tile_scale.reshape(-1),
        hats.reshape(ROWS, NB * K2 * BLK, BLK),
    )
    return out.reshape(64, ROWS, COLS)


def solution(mesh):
    in_specs = (
        P(None, "lat", "lon"),
        P(None, "lat", "lon"),
        P(None, "lat", "lon"),
        P(),
        P(),
        P(),
        P(),
        P(),
        P(),
        P("lat", "lon", None, None),
        P("lat", "lon", None, None),
        P("lat", "lon", None, None, None, None),
    )
    return jax.shard_map(
        shards, mesh=mesh, in_specs=in_specs, out_specs=P(None, "lat", "lon"), check_vma=False)
```

time: 307 us -> 86.9 us (0.28)
  the two profiles are of different devices: /device:TPU:0 before, /device:TPU:4 now
where the time goes in v1:
time: 86.9 us; the launch traced here: 86.3 us
  Pallas kernels  78.7 us (91%)
  local copies, waits for them, and re-layouts  6.58 us (8%)
  other arithmetic  0.95 us (1%)
    pallas_call x1, Pallas kernels, shards(): pl.pallas_call(functools.partial(kernel, n_lon, n_lat), out_shape=jax.Sha...  78.7 us
    unnamed x3, local copies, waits for them, and re-layouts  4.83 us

profile of v1, /device:TPU:4, one launch (start us, length us, event | category | flops | bytes accessed | tf_op | source)
XLA Modules:
  0.0 86.3 jit_solution(7154396787125145651)
XLA Ops:
  0.0 0.9 %fusion = s32[8,4,9,2]{2,3,1,0:T(2,128)S(1)} fusion(s32[8,4,9,2]{2,3,1,0:T(2,128)} %param.21, s32[]{:T(128)S(6)} %mul.15, s32[]{:T(128)S(6)} %mul.12), kind=kLoop, calls=%fused_computation.8 | loop fusion | flops 20736 | bytes 4616 | tf_op jit(solution)/shard_map/add | solution.py:458
  0.9 0.3 copy.14
  1.3 0.7 reshape.28.idx_ref
  2.0 1.1 %copy.15 = f32[8,4,9,2]{3,2,1,0:T(8,128)S(1)} copy(f32[8,4,9,2]{2,3,1,0:T(2,128)} %param.22) | data formatting | bytes 4608 | tf_op args[10]
  3.0 0.7 reshape.29.scale_ref
  3.8 1.9 %copy.16.wm_ref = bf16[9,144,64]{2,1,0:T(8,128)(2,1)} copy(bf16[9,144,64]{1,2,0:T(8,128)(2,1)} %param.17) | data formatting | bytes 331776 | tf_op args[5]
  5.7 78.7 %shard_map.118 = bf16[512,512]{1,0:T(8,128)(2,1)} custom-call(bf16[1568,512]{1,0:T(8,128)(2,1)} %bitcast.8, bf16[512,512]{1,0:T(8,128)(2,1)} %bitcast.10, bf16[512,512]{1,0:T(8,128)(2,1)} %bitcast.11, bf16[9,64,196]{2,1,0:T(8,128)(2,1)} %w1_ref.1, bf16[9,64,64]{2,1,0:T(8,128)(2,1)} %w2_ref.1, bf16[9,144,64]{2,1,0:T(8,128)(2,1)} %copy.16.wm_ref, ...), custom_call_target="tpu_custom_call" | custom-call | tf_op jit(solution)/shard_map/pallas_call | solution.py:463
  84.4 1.9 %copy.18 = bf16[64,8,512]{2,1,0:T(8,128)(2,1)} copy(bf16[64,8,512]{2,1,0:T(8,128)(2,1)} %bitcast.7) | data formatting | bytes 1048576

commit v2 on v1

--- a/solution.py
+++ b/solution.py
@@ -25,7 +25,8 @@
 
 LEFT, RIGHT, UP, DOWN, UL, UR, DL, DR = range(8)
 OPP = (RIGHT, LEFT, DOWN, UP, DR, DL, UR, UL)
-S_OFF, S_SRC, S_SRC_LO, S_SRC_HI, S_CURM, S_CUR, S_PART, S_H1, S_ALM, S_AL, S_T0, S_T1 = range(12)
+(S_OFF, S_SRC, S_SRC_LO, S_SRC_HI, S_CURM, S_CUR, S_PART, S_H1, S_H1_IN, S_ALM, S_AL,
+ S_T0, S_T0_IN, S_T1, S_T1_IN) = range(15)
 
 
 def leaky(v):
@@ -34,9 +35,10 @@
 
 def kernel(
     n_lon, n_lat,
-    off_hbm, cur_hbm, src_hbm, w1_ref, w2_ref, wm_ref, wd_ref, wg_ref, wr_ref,
-    idx_ref, scale_ref, hats_hbm, out_ref,
-    raw_off, raw_src, raw_cur, stage, hats, win, sampled, modulated,
+    off_hbm, cur_hbm, src_hbm, w1_hbm, w2_hbm, wm_hbm, wd_hbm, wg_hbm, wr_hbm,
+    foot_ref, scale_ref, hats_hbm, out_ref,
+    w1_ref, w2_ref, wm_ref, wd_ref, wg_ref, wr_ref,
+    raw_off, raw_src, raw_cur, stage, stage2, hats, win, sampled, modulated,
     v0, h1, h2, joined, t0, i0, t1, i1,
     w1, w2, wm, wd, wg, wr,
     pack_off, got_off, pack_cur, got_cur, pack_al, got_al,
@@ -96,6 +98,14 @@
     load_cur = pltpu.make_async_copy(cur_hbm, raw_cur, load_sem.at[2])
     load_off.start()
     load_src.start()
+    load_weights = [
+        pltpu.make_async_copy(a, b, load_sem.at[3 + n])
+        for n, (a, b) in enumerate((
+            (w1_hbm, w1_ref), (w2_hbm, w2_ref), (wm_hbm, wm_ref), (wd_hbm, wd_ref),
+            (wg_hbm, wg_ref), (wr_hbm, wr_ref)))
+    ]
+    for load in load_weights:
+        load.start()
     load_cur.start()
 
     def hat_load(y):
@@ -107,25 +117,36 @@
     def zero_rows(buf, lo, hi):
         buf[lo:hi] = jnp.zeros((hi - lo,) + buf.shape[1:], buf.dtype)
 
-    for buf, m in ((h1, 2), (joined, 1), (t0, 2), (t1, 2)):
-        zero_rows(buf, 0, m)
-        zero_rows(buf, ROWS + m, ROWS + 2 * m)
-    zero_rows(v0, 0, 1)
-    zero_rows(v0, ROWS + 1, ROWS + 2)
-    part_in[...] = jnp.zeros(part_in.shape, BF)
-    got_cur[...] = jnp.zeros(got_cur.shape, BF)
-    got_al[...] = jnp.zeros(got_al.shape, BF)
-    pack_off[...] = jnp.zeros(pack_off.shape, BF)
-    for i in range(1, ROWS + 1):
-        v0[i, 192:CPAD, :] = jnp.zeros((CPAD - 192, WIDE), BF)
+    def no_halo(top):
+        for buf, m in ((h1, 2), (joined, 1), (t0, 2), (t1, 2)):
+            if top:
+                zero_rows(buf, 0, m)
+            else:
+                zero_rows(buf, ROWS + m, ROWS + 2 * m)
+        n = 0 if top else 1
+        zero_rows(part_in, n, n + 1)
+        for d in (UL, UR) if top else (DL, DR):
+            zero_rows(got_cur, d, d + 1)
+            zero_rows(got_al, d, d + 1)
+
+    pl.when(jnp.logical_not(has_up))(lambda: no_halo(True))
+    pl.when(jnp.logical_not(has_down))(lambda: no_halo(False))
 
     barrier = pltpu.get_barrier_semaphore()
     for d in range(8):
         guarded(nb[d][0], lambda d=d: pl.semaphore_signal(
             barrier, inc=1, device_id=nb[d][1], device_id_type=MESH))
-    both = has_up & has_down
-    pl.when(both)(lambda: pl.semaphore_wait(barrier, 8))
-    pl.when(jnp.logical_not(both))(lambda: pl.semaphore_wait(barrier, 5))
+
+    def all_here():
+        both = has_up & has_down
+        pl.when(both)(lambda: pl.semaphore_wait(barrier, 8))
+        pl.when(jnp.logical_not(both))(lambda: pl.semaphore_wait(barrier, 5))
+
+    zero_rows(v0, 0, 1)
+    zero_rows(v0, ROWS + 1, ROWS + 2)
+    pack_off[...] = jnp.zeros(pack_off.shape, BF)
+    for i in range(1, ROWS + 1):
+        v0[i, 192:CPAD, :] = jnp.zeros((CPAD - 192, WIDE), BF)
 
     lane = lax.broadcasted_iota(jnp.int32, (1, BLK), 1)
 
@@ -144,8 +165,11 @@
         return jnp.where(lane < 8, a, jnp.where(lane >= 120, b, 0.0))
 
     load_off.wait()
-    for j in range(NB):
+    def stage_off(j):
         stage[j] = raw_off[:, j * BLK:(j + 1) * BLK].astype(F32)
+
+    stage_off(0)
+    stage_off(NB - 1)
 
     def staged(channels, y, j):
         return stage[j, pl.ds(y, channels, stride=ROWS), :]
@@ -154,24 +178,18 @@
         [staged(CIN, y, 0) for y in range(ROWS)], 0).astype(BF)
     pack_off[1, 0:CIN, :] = pack_tiles(
         [staged(CIN, y, NB - 1) for y in range(ROWS)], 1).astype(BF)
+    all_here()
     send(S_OFF, LEFT, pack_off.at[0], got_off.at[0])
     send(S_OFF, RIGHT, pack_off.at[1], got_off.at[1])
 
-    def v0_row(y, _):
-        for j in range(NB):
-            v0[y + 1, 0:CIN, j * BLK:(j + 1) * BLK] = staged(CIN, y, j).astype(BF)
-        return 0
-
-    lax.fori_loop(0, ROWS, v0_row, 0)
-
     load_src.wait()
     for j in range(NB):
-        stage[j, 0:512, :] = raw_src[:, j * BLK:(j + 1) * BLK].astype(F32)
+        stage2[j] = raw_src[:, j * BLK:(j + 1) * BLK].astype(F32)
 
     def win_row(y, _):
         for k in range(4):
             for j in range(NB):
-                win[y + 2, j + 2, k * 16:(k + 1) * 16, :] = stage[
+                win[y + 2, j + 2, k * 16:(k + 1) * 16, :] = stage2[
                     j, pl.ds(k * ROWS + y, 16, stride=4 * ROWS), :].astype(BF)
         return 0
 
@@ -183,12 +201,22 @@
     send(S_SRC, LEFT, w_left, win.at[2:10, 6:8])
     send(S_SRC, RIGHT, w_right, win.at[2:10, 0:2])
 
+    for j in range(1, NB - 1):
+        stage_off(j)
+
+    def v0_row(y, _):
+        for j in range(NB):
+            v0[y + 1, 0:CIN, j * BLK:(j + 1) * BLK] = staged(CIN, y, j).astype(BF)
+        return 0
+
+    lax.fori_loop(0, ROWS, v0_row, 0)
+
     load_cur.wait()
     for j in range(NB):
-        stage[j, 512:1024, :] = raw_cur[:, j * BLK:(j + 1) * BLK].astype(F32)
+        stage2[j] = raw_cur[:, j * BLK:(j + 1) * BLK].astype(F32)
 
     def cur_staged(y, j):
-        return stage[j, pl.ds(512 + y, 64, stride=ROWS), :]
+        return stage2[j, pl.ds(y, 64, stride=ROWS), :]
 
     def cur_row(y, _):
         for j in range(NB):
@@ -199,6 +227,8 @@
     pack_cur[0] = pack_tiles([cur_staged(y, 0) for y in range(ROWS)], 0).astype(BF)
     pack_cur[1] = pack_tiles([cur_staged(y, NB - 1) for y in range(ROWS)], 1).astype(BF)
 
+    for load in load_weights:
+        load.wait()
     w1[...] = jnp.zeros(w1.shape, BF)
     for a in range(3):
         for b in range(3):
@@ -209,7 +239,7 @@
         for r in range(4):
             wr[r, b * 64:(b + 1) * 64, :] = jnp.concatenate(
                 [wr_ref[r, 3 * a + b] for a in range(3)], axis=1)
-    wm[...] = jnp.concatenate([wm_ref[t] for t in range(TAPS)], axis=1)
+    wm[...] = wm_ref[...].reshape(TAPS * 64, 144).astype(F32).T.astype(BF)
     row_id = lax.broadcasted_iota(jnp.int32, (64, 64), 0)
     col_id = lax.broadcasted_iota(jnp.int32, (64, 64), 1)
     perm = (row_id == (col_id % 16) * 4 + col_id // 16).astype(BF)
@@ -223,6 +253,21 @@
     def conv_row(src, i, weight):
         x = src[pl.ds(i, 3)].reshape(3 * src.shape[1], WIDE)
         return spread(jnp.dot(weight, x, preferred_element_type=F32))
+
+    def row_out(kind, buf, m, n):
+        send(kind, UP, buf.at[m + n], buf.at[ROWS + m + n])
+        send(kind, DOWN, buf.at[ROWS + m - 1 - n], buf.at[m - 1 - n])
+
+    def row_in(kind, buf, m, n):
+        wait_recv(kind, UP, buf.at[m - 1 - n])
+        wait_recv(kind, DOWN, buf.at[ROWS + m + n])
+
+    def row_sent(kind, buf, m, n):
+        wait_send(kind, UP, buf.at[m + n])
+        wait_send(kind, DOWN, buf.at[ROWS + m - 1 - n])
+
+    def rows_loop(lo, hi, fn):
+        lax.fori_loop(lo, hi, fn, 0, unroll=True)
 
     wait_recv(S_OFF, RIGHT, got_off.at[0])
     wait_recv(S_OFF, LEFT, got_off.at[1])
@@ -238,9 +283,12 @@
         h1[y + 2] = leaky(conv_row(v0, y, w1[...])).astype(BF)
         return 0
 
+    h1_row(1, 0)
+    h1_row(ROWS - 2, 0)
+    row_out(S_H1_IN, h1, 2, 1)
+    rows_loop(2, ROWS - 2, h1_row)
     part_own[0] = conv_row(v0, 0, w1[...])
     part_own[1] = conv_row(v0, ROWS - 1, w1[...])
-    lax.fori_loop(1, ROWS - 1, h1_row, 0)
 
     wait_recv(S_SRC, UP, win.at[0:2, 2:6])
     wait_recv(S_SRC, DOWN, win.at[10:12, 2:6])
@@ -257,19 +305,7 @@
     h1[2] = leaky(part_own[0] + part_in[0].astype(F32)).astype(BF)
     h1[ROWS + 1] = leaky(part_own[1] + part_in[1].astype(F32)).astype(BF)
 
-    def edges_out(kind, buf, count, m):
-        send(kind, UP, buf.at[m:m + count], buf.at[ROWS + m:ROWS + m + count])
-        send(kind, DOWN, buf.at[ROWS + m - count:ROWS + m], buf.at[m - count:m])
-
-    def edges_in(kind, buf, count, m):
-        wait_recv(kind, UP, buf.at[m - count:m])
-        wait_recv(kind, DOWN, buf.at[ROWS + m:ROWS + m + count])
-
-    def edges_sent(kind, buf, count, m):
-        wait_send(kind, UP, buf.at[m:m + count])
-        wait_send(kind, DOWN, buf.at[ROWS + m - count:ROWS + m])
-
-    edges_out(S_H1, h1, 2, 2)
+    row_out(S_H1, h1, 2, 0)
 
     for side, dirs in ((0, (LEFT, UL, DL)), (1, (RIGHT, UR, DR))):
         for d in dirs:
@@ -289,7 +325,7 @@
         h2[y + 1, 128:192] = pltpu.roll(v, WIDE - 1, 1).astype(BF)
         return 0
 
-    lax.fori_loop(1, ROWS - 1, h2_row, 0)
+    rows_loop(1, ROWS - 1, h2_row)
 
     wait_recv(S_SRC, RIGHT, win.at[2:10, 6:8])
     wait_recv(S_SRC, LEFT, win.at[2:10, 0:2])
@@ -304,21 +340,26 @@
     for y in range(ROWS):
         hat_load(y).wait()
 
+    total = NB * n_lon
+    shift = total.bit_length() - 1
+    row_base = lat * ROWS - 2
+    col_base = lon * NB - 2
+
     def sample_row(y, _):
         for j in range(NB):
             for t in range(TAPS):
-                at = (y * NB + j) * K2 + 2 * t
                 parts = []
                 for f in range(2):
-                    ix = idx_ref[at + f]
-                    blk = win[lax.shift_right_logical(ix, 3), lax.bitwise_and(ix, 7)]
-                    parts.append((blk.astype(F32) * scale_ref[at + f]).astype(BF))
+                    ix = foot_ref[y, j, f, t]
+                    row = jnp.clip(lax.shift_right_logical(ix, shift) - row_base, 0, WIN_ROWS - 1)
+                    col = jnp.minimum(lax.bitwise_and(ix - col_base, total - 1), WIN_COLS - 1)
+                    parts.append((win[row, col].astype(F32) * scale_ref[y, j, f, t]).astype(BF))
                 tile = hats[y, (j * K2 + 2 * t) * BLK:(j * K2 + 2 * t + 2) * BLK, :]
                 sampled[y, t * 64:(t + 1) * 64, j * BLK:(j + 1) * BLK] = jnp.dot(
                     jnp.concatenate(parts, axis=1), tile, preferred_element_type=F32)
         return 0
 
-    lax.fori_loop(0, ROWS, sample_row, 0)
+    lax.fori_loop(0, ROWS, sample_row, 0, unroll=2)
 
     def aligned_row(y, _):
         x = h2[pl.ds(y, 3)].reshape(576, WIDE)[:, 0:COLS]
@@ -333,7 +374,7 @@
             wd[...], modulated[...], preferred_element_type=F32).astype(BF)
         return 0
 
-    lax.fori_loop(2, ROWS - 2, aligned_row, 0)
+    rows_loop(2, ROWS - 2, aligned_row)
 
     def edge4(fn):
         return lambda i, c: fn(i + (i // 2) * (ROWS - 4), c)
@@ -341,9 +382,10 @@
     def ring4(fn):
         return lambda i, c: fn(i - 1 + (i // 2) * (ROWS - 2), c)
 
-    edges_in(S_H1, h1, 2, 2)
-    lax.fori_loop(0, 4, ring4(h2_row), 0)
-    lax.fori_loop(0, 4, edge4(aligned_row), 0)
+    row_in(S_H1_IN, h1, 2, 1)
+    row_in(S_H1, h1, 2, 0)
+    rows_loop(0, 4, ring4(h2_row))
+    rows_loop(0, 4, edge4(aligned_row))
 
     send(S_AL, UP, joined.at[1, 64:128, 0:COLS], joined.at[ROWS + 1, 64:128, 0:COLS])
     send(S_AL, DOWN, joined.at[ROWS, 64:128, 0:COLS], joined.at[0, 64:128, 0:COLS])
@@ -390,34 +432,45 @@
     def final_row(y, _):
         trunk = (t1[y + 2].astype(F32) + conv_row(i1, y, wr[3])).astype(BF)
         trunk = trunk[:, 0:COLS].astype(F32)
-        total = trunk + joined[y + 1, 64:128, 0:COLS].astype(F32)
-        for j in range(NB):
-            stage[j, pl.ds(y, 64, stride=ROWS), :] = total[:, j * BLK:(j + 1) * BLK]
-        return 0
-
-    lax.fori_loop(1, ROWS - 1, t0_row, 0)
+        out_ref[y] = (trunk + joined[y + 1, 64:128, 0:COLS].astype(F32)).astype(BF)
+        return 0
+
+    t0_row(1, 0)
+    t0_row(ROWS - 2, 0)
+    row_out(S_T0_IN, t0, 2, 1)
+    rows_loop(2, ROWS - 2, t0_row)
     wait_recv(S_CUR, UP, joined.at[0, 0:64, 0:COLS])
     wait_recv(S_CUR, DOWN, joined.at[ROWS + 1, 0:64, 0:COLS])
     wait_recv(S_AL, UP, joined.at[0, 64:128, 0:COLS])
     wait_recv(S_AL, DOWN, joined.at[ROWS + 1, 64:128, 0:COLS])
     t0_row(0, 0)
     t0_row(ROWS - 1, 0)
-    edges_out(S_T0, t0, 2, 2)
+    row_out(S_T0, t0, 2, 0)
     inner0 = inner_row(i0, t0, 0)
     inner1 = inner_row(i1, t1, 2)
-    lax.fori_loop(1, ROWS - 1, inner0, 0)
-    lax.fori_loop(2, ROWS - 2, t1_row, 0)
-    edges_in(S_T0, t0, 2, 2)
-    lax.fori_loop(0, 4, ring4(inner0), 0)
-    lax.fori_loop(0, 4, edge4(t1_row), 0)
-    edges_out(S_T1, t1, 2, 2)
-    lax.fori_loop(1, ROWS - 1, inner1, 0)
-    lax.fori_loop(2, ROWS - 2, final_row, 0)
-    edges_in(S_T1, t1, 2, 2)
-    lax.fori_loop(0, 4, ring4(inner1), 0)
-    lax.fori_loop(0, 4, edge4(final_row), 0)
-    for j in range(NB):
-        out_ref[:, j * BLK:(j + 1) * BLK] = stage[j, 0:512, :].astype(BF)
+    rows_loop(1, ROWS - 1, inner0)
+    rows_loop(2, ROWS - 2, t1_row)
+    row_in(S_T0_IN, t0, 2, 1)
+    row_in(S_T0, t0, 2, 0)
+    rows_loop(0, 4, ring4(inner0))
+    t1_row(0, 0)
+    t1_row(ROWS - 1, 0)
+    row_out(S_T1, t1, 2, 0)
+    t1_row(1, 0)
+    t1_row(ROWS - 2, 0)
+    row_out(S_T1_IN, t1, 2, 1)
+    rows_loop(1, ROWS - 1, inner1)
+    rows_loop(2, ROWS - 2, final_row)
+    row_in(S_T1, t1, 2, 0)
+    inner1(0, 0)
+    inner1(ROWS - 1, 0)
+    final_row(1, 0)
+    final_row(ROWS - 2, 0)
+    row_in(S_T1_IN, t1, 2, 1)
+    inner1(-1, 0)
+    inner1(ROWS, 0)
+    final_row(0, 0)
+    final_row(ROWS - 1, 0)
 
     wait_send(S_OFF, LEFT, pack_off.at[0])
     wait_send(S_OFF, RIGHT, pack_off.at[1])
@@ -442,9 +495,9 @@
     wait_send(S_CUR, DOWN, joined.at[ROWS, 0:64, 0:COLS])
     wait_send(S_AL, UP, joined.at[1, 64:128, 0:COLS])
     wait_send(S_AL, DOWN, joined.at[ROWS, 64:128, 0:COLS])
-    edges_sent(S_H1, h1, 2, 2)
-    edges_sent(S_T0, t0, 2, 2)
-    edges_sent(S_T1, t1, 2, 2)
+    for kind, buf in ((S_H1, h1), (S_T0, t0), (S_T1, t1)):
+        row_sent(kind, buf, 2, 0)
+        row_sent(kind + 1, buf, 2, 1)
 
 
 def shards(
@@ -452,22 +505,22 @@
     merge_weight, residual_weight, footprint, tile_scale, hats,
 ):
     n_lon, n_lat = lax.axis_size("lon"), lax.axis_size("lat")
-    total_blocks = NB * n_lon
-    row = footprint // total_blocks - lax.axis_index("lat") * ROWS + 2
-    col = (footprint % total_blocks - lax.axis_index("lon") * NB + 2) % total_blocks
-    index = (row * WIN_COLS + col).reshape(-1)
+    assert n_lon & (n_lon - 1) == 0
     vmem = pl.BlockSpec(memory_space=pltpu.VMEM)
     smem = pl.BlockSpec(memory_space=pltpu.SMEM)
     hbm = pl.BlockSpec(memory_space=pl.ANY)
     V = pltpu.VMEM
     out = pl.pallas_call(
         functools.partial(kernel, n_lon, n_lat),
-        out_shape=jax.ShapeDtypeStruct((64 * ROWS, COLS), BF),
-        in_specs=[hbm, hbm, hbm] + [vmem] * 6 + [smem, smem, hbm],
+        out_shape=jax.ShapeDtypeStruct((ROWS, 64, COLS), BF),
+        in_specs=[hbm] * 9 + [smem, smem, hbm],
         out_specs=vmem,
         scratch_shapes=[
+            V((9, 64, CIN), BF), V((9, 64, 64), BF), V((9, 64, 144), BF), V((9, 64, 64), BF),
+            V((9, 64, 128), BF), V((4, 9, 64, 64), BF),
             V((CIN * ROWS, COLS), BF), V((64 * ROWS, COLS), BF), V((64 * ROWS, COLS), BF),
             V((NB, CIN * ROWS, BLK), F32),
+            V((NB, 64 * ROWS, BLK), F32),
             V((ROWS, NB * K2 * BLK, BLK), BF),
             V((WIN_ROWS, WIN_COLS, 64, BLK), BF),
             V((ROWS, TAPS * 64, COLS), F32),
@@ -486,10 +539,10 @@
             V((2, 64, BLK), BF), V((8, 64, BLK), BF),
             V((2, 64, BLK), BF), V((8, 64, BLK), BF),
             V((2, 64, WIDE), BF), V((2, 64, WIDE), BF), V((2, 64, WIDE), F32),
-            pltpu.SemaphoreType.DMA((3,)),
+            pltpu.SemaphoreType.DMA((9,)),
             pltpu.SemaphoreType.DMA((ROWS,)),
-            pltpu.SemaphoreType.DMA((12, 8)),
-            pltpu.SemaphoreType.DMA((12, 8)),
+            pltpu.SemaphoreType.DMA((15, 8)),
+            pltpu.SemaphoreType.DMA((15, 8)),
         ],
         compiler_params=pltpu.CompilerParams(
             collective_id=0, has_side_effects=True, vmem_limit_bytes=60 * 2**20),
@@ -497,12 +550,12 @@
         offset_input.reshape(CIN * ROWS, COLS),
         current.reshape(64 * ROWS, COLS),
         source.reshape(64 * ROWS, COLS),
-        first_weight, second_weight, mask_weight, deform_weight, merge_weight,
+        first_weight, second_weight, mask_weight.transpose(0, 2, 1), deform_weight, merge_weight,
         residual_weight.reshape(4, 9, 64, 64),
-        index, tile_scale.reshape(-1),
+        footprint.transpose(0, 1, 3, 2), tile_scale.transpose(0, 1, 3, 2),
         hats.reshape(ROWS, NB * K2 * BLK, BLK),
     )
-    return out.reshape(64, ROWS, COLS)
+    return out.transpose(1, 0, 2)
 
 
 def solution(mesh):

time: 86.9 us -> 72.9 us (0.84)
  Pallas kernels: 78.7 us -> 70.2 us
  local copies, waits for them, and re-layouts: 6.58 us -> 2.13 us
  other arithmetic: 0.95 us -> 0 us
    pallas_call x1, Pallas kernels: 78.7 us -> 70.2 us  [shards(): pl.pallas_call(functools.partial(kernel, n_lon, n_lat), out_shape=jax.Sha...]
    unnamed x3 -> x0, local copies, waits for them, and re-layouts: 4.83 us -> none
    transpose x0 -> x1, local copies, waits for them, and re-layouts: none -> 2.13 us  [shards(): return out.transpose(1, 0, 2)]
    reshape x2 -> x0, local copies, waits for them, and re-layouts: 1.44 us -> none  [the longest x1 0.73 us: shards(): index = (row * WIN_COLS + col).reshape(-1)]
    add x1 -> x0, other arithmetic: 0.95 us -> none  [shards(): index = (row * WIN_COLS + col).reshape(-1)]
where the time goes in v2:
time: 72.9 us; the launch traced here: 72.3 us
  Pallas kernels  70.2 us (96%)
  local copies, waits for them, and re-layouts  2.13 us (3%)
    pallas_call x1, Pallas kernels, shards(): pl.pallas_call(functools.partial(kernel, n_lon, n_lat), out_shape=jax.Sha...  70.2 us
    transpose x1, local copies, waits for them, and re-layouts, shards(): return out.transpose(1, 0, 2)  2.13 us

profile of v2, /device:TPU:4, one launch (start us, length us, event | category | flops | bytes accessed | tf_op | source)
XLA Modules:
  0.0 72.3 jit_solution(14434563505332251998)
XLA Ops:
  0.0 70.2 %shard_map.118 = bf16[8,64,512]{2,1,0:T(8,128)(2,1)} custom-call(bf16[1568,512]{1,0:T(8,128)(2,1)} %bitcast.11, bf16[512,512]{1,0:T(8,128)(2,1)} %bitcast.13, bf16[512,512]{1,0:T(8,128)(2,1)} %bitcast.14, bf16[9,64,196]{2,1,0:T(8,128)(2,1)} %w1_hbm.1, bf16[9,64,64]{2,1,0:T(8,128)(2,1)} %w2_hbm.1, bf16[9,64,144]{2,1,0:T(8,128)(2,1)} %bitcast.15, ...), custom_call_target="tpu_custom_call" | custom-call | tf_op jit(solution)/shard_map/pallas_call | solution.py:513
  70.2 2.1 %copy.13 = bf16[64,8,512]{2,1,0:T(8,128)(2,1)} copy(bf16[64,8,512]{2,0,1:T(8,128)(2,1)} %bitcast.10) | data formatting | bytes 1048576 | tf_op jit(solution)/shard_map/transpose | solution.py:558

commit v3 on v2

--- a/solution.py
+++ b/solution.py
@@ -36,14 +36,15 @@
 def kernel(
     n_lon, n_lat,
     off_hbm, cur_hbm, src_hbm, w1_hbm, w2_hbm, wm_hbm, wd_hbm, wg_hbm, wr_hbm,
-    foot_ref, scale_ref, hats_hbm, out_ref,
+    foot_hbm, scale_hbm, hats_hbm, out_hbm,
+    foot_ref, scale_ref, out_ref,
     w1_ref, w2_ref, wm_ref, wd_ref, wg_ref, wr_ref,
-    raw_off, raw_src, raw_cur, stage, stage2, hats, win, sampled, modulated,
+    raw_off, raw_src, raw_cur, stage, stage2, hats, near, win, sampled, modulated,
     v0, h1, h2, joined, t0, i0, t1, i1,
     w1, w2, wm, wd, wg, wr,
     pack_off, got_off, pack_cur, got_cur, pack_al, got_al,
     part_out, part_in, part_own,
-    load_sem, hat_sem, send_sem, recv_sem,
+    load_sem, hat_sem, out_sem, send_sem, recv_sem,
 ):
     lon = lax.axis_index("lon")
     lat = lax.axis_index("lat")
@@ -102,7 +103,7 @@
         pltpu.make_async_copy(a, b, load_sem.at[3 + n])
         for n, (a, b) in enumerate((
             (w1_hbm, w1_ref), (w2_hbm, w2_ref), (wm_hbm, wm_ref), (wd_hbm, wd_ref),
-            (wg_hbm, wg_ref), (wr_hbm, wr_ref)))
+            (wg_hbm, wg_ref), (wr_hbm, wr_ref), (foot_hbm, foot_ref), (scale_hbm, scale_ref)))
     ]
     for load in load_weights:
         load.start()
@@ -189,17 +190,109 @@
     def win_row(y, _):
         for k in range(4):
             for j in range(NB):
-                win[y + 2, j + 2, k * 16:(k + 1) * 16, :] = stage2[
+                near[y, j + 2, k * 16:(k + 1) * 16, :] = stage2[
                     j, pl.ds(k * ROWS + y, 16, stride=4 * ROWS), :].astype(BF)
         return 0
 
     lax.fori_loop(0, ROWS, win_row, 0)
-    w_lat_up, w_lat_dn = win.at[2:4, 2:6], win.at[8:10, 2:6]
-    send(S_SRC, UP, w_lat_up, win.at[10:12, 2:6])
-    send(S_SRC, DOWN, w_lat_dn, win.at[0:2, 2:6])
-    w_left, w_right = win.at[2:10, 2:4], win.at[2:10, 4:6]
-    send(S_SRC, LEFT, w_left, win.at[2:10, 6:8])
-    send(S_SRC, RIGHT, w_right, win.at[2:10, 0:2])
+
+    def by_reach(row_tile, fn):
+        outer = (row_tile < n_lat // 4) | (row_tile >= n_lat - n_lat // 4)
+        pl.when(outer)(lambda: fn(2))
+        pl.when(jnp.logical_not(outer))(lambda: fn(1))
+
+    def to_left(rows, n, buf=win):
+        return buf.at[rows, 2:2 + n]
+
+    def to_right(rows, n, buf=win):
+        return buf.at[rows, 6 - n:6]
+
+    def from_left(rows, n, buf=win):
+        return buf.at[rows, 2 - n:2]
+
+    def from_right(rows, n, buf=win):
+        return buf.at[rows, 6:6 + n]
+
+    INNER, TOP, BOTTOM = slice(0, 8), slice(0, 2), slice(10, 12)
+    FIRST, LAST = slice(0, 2), slice(6, 8)
+    odd = lax.rem(lon, 2) == 1
+    even = jnp.logical_not(odd)
+
+    def source_columns(n):
+        send(S_SRC, LEFT, to_left(INNER, n, near), from_right(INNER, n, near))
+        send(S_SRC, RIGHT, to_right(INNER, n, near), from_left(INNER, n, near))
+
+    def source_columns_in(n):
+        wait_recv(S_SRC, RIGHT, from_right(INNER, n, near))
+        wait_recv(S_SRC, LEFT, from_left(INNER, n, near))
+
+    def source_columns_sent(n):
+        wait_send(S_SRC, LEFT, to_left(INNER, n, near))
+        wait_send(S_SRC, RIGHT, to_right(INNER, n, near))
+
+    def source_rows():
+        send(S_SRC, UP, near.at[FIRST, 2:6], win.at[BOTTOM, 2:6])
+        send(S_SRC, DOWN, near.at[LAST, 2:6], win.at[TOP, 2:6])
+
+        @pl.when(even)
+        def _():
+            by_reach(lat - 1, lambda n: send(S_SRC, UL, to_left(FIRST, n, near), from_right(BOTTOM, n)))
+            by_reach(lat + 1, lambda n: send(S_SRC, DL, to_left(LAST, n, near), from_right(TOP, n)))
+
+        @pl.when(odd)
+        def _():
+            by_reach(lat - 1, lambda n: send(S_SRC, UR, to_right(FIRST, n, near), from_left(BOTTOM, n)))
+            by_reach(lat + 1, lambda n: send(S_SRC, DR, to_right(LAST, n, near), from_left(TOP, n)))
+
+    def source_rows_sent():
+        wait_send(S_SRC, UP, near.at[FIRST, 2:6])
+        wait_send(S_SRC, DOWN, near.at[LAST, 2:6])
+
+        @pl.when(even)
+        def _():
+            by_reach(lat - 1, lambda n: wait_send(S_SRC, UL, to_left(FIRST, n, near)))
+            by_reach(lat + 1, lambda n: wait_send(S_SRC, DL, to_left(LAST, n, near)))
+
+        @pl.when(odd)
+        def _():
+            by_reach(lat - 1, lambda n: wait_send(S_SRC, UR, to_right(FIRST, n, near)))
+            by_reach(lat + 1, lambda n: wait_send(S_SRC, DR, to_right(LAST, n, near)))
+
+    def relay(kind, rows, n):
+        pl.when(even)(lambda: send(kind, RIGHT, to_right(rows, n), from_left(rows, n)))
+        pl.when(odd)(lambda: send(kind, LEFT, to_left(rows, n), from_right(rows, n)))
+
+    def relay_in(kind, rows, n):
+        pl.when(even)(lambda: wait_recv(kind, RIGHT, from_right(rows, n)))
+        pl.when(odd)(lambda: wait_recv(kind, LEFT, from_left(rows, n)))
+
+    def relay_sent(kind, rows, n):
+        pl.when(even)(lambda: wait_send(kind, RIGHT, to_right(rows, n)))
+        pl.when(odd)(lambda: wait_send(kind, LEFT, to_left(rows, n)))
+
+    def each_relay(fn):
+        pl.when(has_up)(lambda: by_reach(lat, lambda n: fn(S_SRC_LO, TOP, n)))
+        pl.when(has_down)(lambda: by_reach(lat, lambda n: fn(S_SRC_HI, BOTTOM, n)))
+
+    def source_rows_in():
+        wait_recv(S_SRC, UP, win.at[TOP, 2:6])
+        wait_recv(S_SRC, DOWN, win.at[BOTTOM, 2:6])
+        each_relay(relay)
+
+    def source_corners_in():
+        @pl.when(odd)
+        def _():
+            by_reach(lat, lambda n: wait_recv(S_SRC, UR, from_right(TOP, n)))
+            by_reach(lat, lambda n: wait_recv(S_SRC, DR, from_right(BOTTOM, n)))
+
+        @pl.when(even)
+        def _():
+            by_reach(lat, lambda n: wait_recv(S_SRC, UL, from_left(TOP, n)))
+            by_reach(lat, lambda n: wait_recv(S_SRC, DL, from_left(BOTTOM, n)))
+
+        each_relay(relay_in)
+
+    by_reach(lat, source_columns)
 
     for j in range(1, NB - 1):
         stage_off(j)
@@ -269,6 +362,12 @@
     def rows_loop(lo, hi, fn):
         lax.fori_loop(lo, hi, fn, 0, unroll=True)
 
+    def edge4(fn):
+        return lambda i, c: fn(i + (i // 2) * (ROWS - 4), c)
+
+    def ring4(fn):
+        return lambda i, c: fn(i - 1 + (i // 2) * (ROWS - 2), c)
+
     wait_recv(S_OFF, RIGHT, got_off.at[0])
     wait_recv(S_OFF, LEFT, got_off.at[1])
     for y in range(ROWS):
@@ -278,6 +377,7 @@
     part_out[1] = spread(jnp.dot(w1[:, :CPAD], v0[ROWS], preferred_element_type=F32)).astype(BF)
     send(S_PART, UP, part_out.at[0], part_in.at[1])
     send(S_PART, DOWN, part_out.at[1], part_in.at[0])
+    source_rows()
 
     def h1_row(y, _):
         h1[y + 2] = leaky(conv_row(v0, y, w1[...])).astype(BF)
@@ -290,15 +390,29 @@
     part_own[0] = conv_row(v0, 0, w1[...])
     part_own[1] = conv_row(v0, ROWS - 1, w1[...])
 
-    wait_recv(S_SRC, UP, win.at[0:2, 2:6])
-    wait_recv(S_SRC, DOWN, win.at[10:12, 2:6])
-
-    def relay(kind, rows):
-        send(kind, LEFT, win.at[rows, 2:4], win.at[rows, 6:8])
-        send(kind, RIGHT, win.at[rows, 4:6], win.at[rows, 0:2])
-
-    pl.when(has_up)(lambda: relay(S_SRC_LO, slice(0, 2)))
-    pl.when(has_down)(lambda: relay(S_SRC_HI, slice(10, 12)))
+    total = NB * n_lon
+    shift = total.bit_length() - 1
+    col_base = lon * NB - 2
+
+    def sample_row(y, src, first, count):
+        for j in range(NB):
+            for t in range(TAPS):
+                parts = []
+                for f in range(2):
+                    ix = foot_ref[y, j, f, t]
+                    row = jnp.clip(lax.shift_right_logical(ix, shift) - first, 0, count - 1)
+                    col = jnp.minimum(lax.bitwise_and(ix - col_base, total - 1), WIN_COLS - 1)
+                    parts.append((src[row, col].astype(F32) * scale_ref[y, j, f, t]).astype(BF))
+                tile = hats[y, (j * K2 + 2 * t) * BLK:(j * K2 + 2 * t + 2) * BLK, :]
+                sampled[y, t * 64:(t + 1) * 64, j * BLK:(j + 1) * BLK] = jnp.dot(
+                    jnp.concatenate(parts, axis=1), tile, preferred_element_type=F32)
+        return 0
+
+    by_reach(lat, source_columns_in)
+    for y in range(2, ROWS - 2):
+        hat_load(y).wait()
+    rows_loop(2, ROWS - 2, lambda y, _: sample_row(y, near, lat * ROWS, ROWS))
+    win[2:2 + ROWS] = near[...]
 
     wait_recv(S_PART, UP, part_in.at[0])
     wait_recv(S_PART, DOWN, part_in.at[1])
@@ -327,39 +441,11 @@
 
     rows_loop(1, ROWS - 1, h2_row)
 
-    wait_recv(S_SRC, RIGHT, win.at[2:10, 6:8])
-    wait_recv(S_SRC, LEFT, win.at[2:10, 0:2])
-
-    def relayed(kind, rows):
-        wait_recv(kind, RIGHT, win.at[rows, 6:8])
-        wait_recv(kind, LEFT, win.at[rows, 0:2])
-
-    pl.when(has_up)(lambda: relayed(S_SRC_LO, slice(0, 2)))
-    pl.when(has_down)(lambda: relayed(S_SRC_HI, slice(10, 12)))
-
-    for y in range(ROWS):
+    source_rows_in()
+    source_corners_in()
+    for y in (0, 1, ROWS - 2, ROWS - 1):
         hat_load(y).wait()
-
-    total = NB * n_lon
-    shift = total.bit_length() - 1
-    row_base = lat * ROWS - 2
-    col_base = lon * NB - 2
-
-    def sample_row(y, _):
-        for j in range(NB):
-            for t in range(TAPS):
-                parts = []
-                for f in range(2):
-                    ix = foot_ref[y, j, f, t]
-                    row = jnp.clip(lax.shift_right_logical(ix, shift) - row_base, 0, WIN_ROWS - 1)
-                    col = jnp.minimum(lax.bitwise_and(ix - col_base, total - 1), WIN_COLS - 1)
-                    parts.append((win[row, col].astype(F32) * scale_ref[y, j, f, t]).astype(BF))
-                tile = hats[y, (j * K2 + 2 * t) * BLK:(j * K2 + 2 * t + 2) * BLK, :]
-                sampled[y, t * 64:(t + 1) * 64, j * BLK:(j + 1) * BLK] = jnp.dot(
-                    jnp.concatenate(parts, axis=1), tile, preferred_element_type=F32)
-        return 0
-
-    lax.fori_loop(0, ROWS, sample_row, 0, unroll=2)
+    rows_loop(0, 4, edge4(lambda y, _: sample_row(y, win, lat * ROWS - 2, WIN_ROWS)))
 
     def aligned_row(y, _):
         x = h2[pl.ds(y, 3)].reshape(576, WIDE)[:, 0:COLS]
@@ -376,12 +462,6 @@
 
     rows_loop(2, ROWS - 2, aligned_row)
 
-    def edge4(fn):
-        return lambda i, c: fn(i + (i // 2) * (ROWS - 4), c)
-
-    def ring4(fn):
-        return lambda i, c: fn(i - 1 + (i // 2) * (ROWS - 2), c)
-
     row_in(S_H1_IN, h1, 2, 1)
     row_in(S_H1, h1, 2, 0)
     rows_loop(0, 4, ring4(h2_row))
@@ -429,10 +509,14 @@
         t1[y + 2] = (t0[y + 2].astype(F32) + conv_row(i0, y, wr[1])).astype(BF)
         return 0
 
+    def out_copy(y):
+        return pltpu.make_async_copy(out_ref.at[y], out_hbm.at[y], out_sem.at[y])
+
     def final_row(y, _):
         trunk = (t1[y + 2].astype(F32) + conv_row(i1, y, wr[3])).astype(BF)
         trunk = trunk[:, 0:COLS].astype(F32)
         out_ref[y] = (trunk + joined[y + 1, 64:128, 0:COLS].astype(F32)).astype(BF)
+        out_copy(y).start()
         return 0
 
     t0_row(1, 0)
@@ -472,19 +556,13 @@
     final_row(0, 0)
     final_row(ROWS - 1, 0)
 
+    for y in range(ROWS):
+        out_copy(y).wait()
     wait_send(S_OFF, LEFT, pack_off.at[0])
     wait_send(S_OFF, RIGHT, pack_off.at[1])
-    wait_send(S_SRC, UP, w_lat_up)
-    wait_send(S_SRC, DOWN, w_lat_dn)
-    wait_send(S_SRC, LEFT, w_left)
-    wait_send(S_SRC, RIGHT, w_right)
-
-    def relay_sent(kind, rows):
-        wait_send(kind, LEFT, win.at[rows, 2:4])
-        wait_send(kind, RIGHT, win.at[rows, 4:6])
-
-    pl.when(has_up)(lambda: relay_sent(S_SRC_LO, slice(0, 2)))
-    pl.when(has_down)(lambda: relay_sent(S_SRC_HI, slice(10, 12)))
+    by_reach(lat, source_columns_sent)
+    source_rows_sent()
+    each_relay(relay_sent)
     wait_send(S_PART, UP, part_out.at[0])
     wait_send(S_PART, DOWN, part_out.at[1])
     for side, dirs in ((0, (LEFT, UL, DL)), (1, (RIGHT, UR, DR))):
@@ -506,22 +584,23 @@
 ):
     n_lon, n_lat = lax.axis_size("lon"), lax.axis_size("lat")
     assert n_lon & (n_lon - 1) == 0
-    vmem = pl.BlockSpec(memory_space=pltpu.VMEM)
-    smem = pl.BlockSpec(memory_space=pltpu.SMEM)
     hbm = pl.BlockSpec(memory_space=pl.ANY)
     V = pltpu.VMEM
     out = pl.pallas_call(
         functools.partial(kernel, n_lon, n_lat),
         out_shape=jax.ShapeDtypeStruct((ROWS, 64, COLS), BF),
-        in_specs=[hbm] * 9 + [smem, smem, hbm],
-        out_specs=vmem,
+        in_specs=[hbm] * 12,
+        out_specs=hbm,
         scratch_shapes=[
+            pltpu.SMEM((ROWS, NB, 2, TAPS), jnp.int32), pltpu.SMEM((ROWS, NB, 2, TAPS), F32),
+            V((ROWS, 64, COLS), BF),
             V((9, 64, CIN), BF), V((9, 64, 64), BF), V((9, 64, 144), BF), V((9, 64, 64), BF),
             V((9, 64, 128), BF), V((4, 9, 64, 64), BF),
             V((CIN * ROWS, COLS), BF), V((64 * ROWS, COLS), BF), V((64 * ROWS, COLS), BF),
             V((NB, CIN * ROWS, BLK), F32),
             V((NB, 64 * ROWS, BLK), F32),
             V((ROWS, NB * K2 * BLK, BLK), BF),
+            V((ROWS, WIN_COLS, 64, BLK), BF),
             V((WIN_ROWS, WIN_COLS, 64, BLK), BF),
             V((ROWS, TAPS * 64, COLS), F32),
             V((TAPS * 64, COLS), BF),
@@ -539,7 +618,8 @@
             V((2, 64, BLK), BF), V((8, 64, BLK), BF),
             V((2, 64, BLK), BF), V((8, 64, BLK), BF),
             V((2, 64, WIDE), BF), V((2, 64, WIDE), BF), V((2, 64, WIDE), F32),
-            pltpu.SemaphoreType.DMA((9,)),
+            pltpu.SemaphoreType.DMA((11,)),
+            pltpu.SemaphoreType.DMA((ROWS,)),
             pltpu.SemaphoreType.DMA((ROWS,)),
             pltpu.SemaphoreType.DMA((15, 8)),
             pltpu.SemaphoreType.DMA((15, 8)),

time: 72.9 us -> 65.5 us (0.90)
  Pallas kernels: 70.2 us -> 63.3 us
    pallas_call x1, Pallas kernels: 70.2 us -> 63.3 us  [shards(): pl.pallas_call(functools.partial(kernel, n_lon, n_lat), out_shape=jax.Sha...]
where the time goes in v3:
time: 65.5 us; the launch traced here: 65.4 us
  Pallas kernels  63.3 us (97%)
  local copies, waits for them, and re-layouts  2.13 us (3%)
    pallas_call x1, Pallas kernels, shards(): pl.pallas_call(functools.partial(kernel, n_lon, n_lat), out_shape=jax.Sha...  63.3 us
    transpose x1, local copies, waits for them, and re-layouts, shards(): return out.transpose(1, 0, 2)  2.13 us

profile of v3, /device:TPU:4, one launch (start us, length us, event | category | flops | bytes accessed | tf_op | source)
XLA Modules:
  0.0 65.4 jit_solution(15947794134700743329)
XLA Ops:
  0.0 63.3 %shard_map.118 = bf16[8,64,512]{2,1,0:T(8,128)(2,1)} custom-call(bf16[1568,512]{1,0:T(8,128)(2,1)} %bitcast.11, bf16[512,512]{1,0:T(8,128)(2,1)} %bitcast.13, bf16[512,512]{1,0:T(8,128)(2,1)} %bitcast.14, bf16[9,64,196]{2,1,0:T(8,128)(2,1)} %w1_hbm.1, bf16[9,64,64]{2,1,0:T(8,128)(2,1)} %w2_hbm.1, bf16[9,64,144]{2,1,0:T(8,128)(2,1)} %bitcast.15, ...), custom_call_target="tpu_custom_call" | custom-call | tf_op jit(solution)/shard_map/pallas_call | solution.py:589
  63.3 2.1 %copy.13 = bf16[64,8,512]{2,1,0:T(8,128)(2,1)} copy(bf16[64,8,512]{2,0,1:T(8,128)(2,1)} %bitcast.10) | data formatting | bytes 1048576 | tf_op jit(solution)/shard_map/transpose | solution.py:638

commit v4 on v3

--- a/solution.py
+++ b/solution.py
@@ -24,9 +24,11 @@
 K2 = 18
 
 LEFT, RIGHT, UP, DOWN, UL, UR, DL, DR = range(8)
+AL_CORNERS = ((0, UL), (0, UR), (1, DL), (1, DR))
 OPP = (RIGHT, LEFT, DOWN, UP, DR, DL, UR, UL)
 (S_OFF, S_SRC, S_SRC_LO, S_SRC_HI, S_CURM, S_CUR, S_PART, S_H1, S_H1_IN, S_ALM, S_AL,
  S_T0, S_T0_IN, S_T1, S_T1_IN) = range(15)
+KINDS = 15
 
 
 def leaky(v):
@@ -42,8 +44,8 @@
     raw_off, raw_src, raw_cur, stage, stage2, hats, near, win, sampled, modulated,
     v0, h1, h2, joined, t0, i0, t1, i1,
     w1, w2, wm, wd, wg, wr,
-    pack_off, got_off, pack_cur, got_cur, pack_al, got_al,
-    part_out, part_in, part_own,
+    pack_off, got_off, pack_cur, got_cur, pack_al, got_al, got_corner,
+    part_out, part_in, part_own, sq_out, sq_in,
     load_sem, hat_sem, out_sem, send_sem, recv_sem,
 ):
     lon = lax.axis_index("lon")
@@ -94,10 +96,19 @@
             ).wait_recv()
         guarded(nb[direction][0], go)
 
-    load_off = pltpu.make_async_copy(off_hbm, raw_off, load_sem.at[0])
+    barrier = pltpu.get_barrier_semaphore()
+    for d in range(8):
+        guarded(nb[d][0], lambda d=d: pl.semaphore_signal(
+            barrier, inc=1, device_id=nb[d][1], device_id_type=MESH))
+
+    def off_load(lo, hi, n):
+        return pltpu.make_async_copy(off_hbm.at[:, lo:hi], raw_off.at[:, lo:hi], load_sem.at[n])
+
+    load_off = [off_load(0, BLK, 0), off_load(COLS - BLK, COLS, 11), off_load(BLK, COLS - BLK, 12)]
     load_src = pltpu.make_async_copy(src_hbm, raw_src, load_sem.at[1])
     load_cur = pltpu.make_async_copy(cur_hbm, raw_cur, load_sem.at[2])
-    load_off.start()
+    for load in load_off:
+        load.start()
     load_src.start()
     load_weights = [
         pltpu.make_async_copy(a, b, load_sem.at[3 + n])
@@ -112,9 +123,6 @@
     def hat_load(y):
         return pltpu.make_async_copy(hats_hbm.at[y], hats.at[y], hat_sem.at[y])
 
-    for y in range(ROWS):
-        hat_load(y).start()
-
     def zero_rows(buf, lo, hi):
         buf[lo:hi] = jnp.zeros((hi - lo,) + buf.shape[1:], buf.dtype)
 
@@ -126,17 +134,9 @@
                 zero_rows(buf, ROWS + m, ROWS + 2 * m)
         n = 0 if top else 1
         zero_rows(part_in, n, n + 1)
-        for d in (UL, UR) if top else (DL, DR):
-            zero_rows(got_cur, d, d + 1)
-            zero_rows(got_al, d, d + 1)
 
     pl.when(jnp.logical_not(has_up))(lambda: no_halo(True))
     pl.when(jnp.logical_not(has_down))(lambda: no_halo(False))
-
-    barrier = pltpu.get_barrier_semaphore()
-    for d in range(8):
-        guarded(nb[d][0], lambda d=d: pl.semaphore_signal(
-            barrier, inc=1, device_id=nb[d][1], device_id_type=MESH))
 
     def all_here():
         both = has_up & has_down
@@ -165,7 +165,45 @@
         b = pltpu.roll(from_left, 120 - 8 * y, 1)
         return jnp.where(lane < 8, a, jnp.where(lane >= 120, b, 0.0))
 
-    load_off.wait()
+    def squeeze(tile):
+        total = jnp.zeros((16, BLK), F32)
+        for k in range(4):
+            moved = pltpu.roll(tile[16 * k:16 * k + 16], 16 * k + 8, 1)
+            total = jnp.where((lane >= 16 * k) & (lane < 16 * k + 16), moved, total)
+        return total.astype(BF)
+
+    def expand(small, k):
+        return pltpu.roll(small.astype(F32), 120 - 16 * k, 1)
+
+    def put_margin(row, small):
+        for k in range(4):
+            wide = jnp.where((lane < 8) | (lane >= 120), expand(small, k), 0.0)
+            row[16 * k:16 * k + 16, COLS:WIDE] = wide.astype(BF)
+
+    def rows_send(kind, up_row, up_dst, down_row, down_dst):
+        send(kind, UP, up_row.at[:, 0:COLS], up_dst.at[:, 0:COLS])
+        send(kind, DOWN, down_row.at[:, 0:COLS], down_dst.at[:, 0:COLS])
+        sq_out[kind, 0] = squeeze(up_row[:, COLS:WIDE].astype(F32))
+        sq_out[kind, 1] = squeeze(down_row[:, COLS:WIDE].astype(F32))
+        send(kind + KINDS, UP, sq_out.at[kind, 0], sq_in.at[kind, 1])
+        send(kind + KINDS, DOWN, sq_out.at[kind, 1], sq_in.at[kind, 0])
+
+    def rows_recv(kind, up_dst, down_dst):
+        wait_recv(kind + KINDS, UP, sq_in.at[kind, 0])
+        wait_recv(kind + KINDS, DOWN, sq_in.at[kind, 1])
+        wait_recv(kind, UP, up_dst.at[:, 0:COLS])
+        wait_recv(kind, DOWN, down_dst.at[:, 0:COLS])
+        pl.when(has_up)(lambda: put_margin(up_dst, sq_in[kind, 0]))
+        pl.when(has_down)(lambda: put_margin(down_dst, sq_in[kind, 1]))
+
+    def rows_sent(kind, up_row, down_row):
+        wait_send(kind, UP, up_row.at[:, 0:COLS])
+        wait_send(kind, DOWN, down_row.at[:, 0:COLS])
+        wait_send(kind + KINDS, UP, sq_out.at[kind, 0])
+        wait_send(kind + KINDS, DOWN, sq_out.at[kind, 1])
+
+    load_off[0].wait()
+    load_off[1].wait()
     def stage_off(j):
         stage[j] = raw_off[:, j * BLK:(j + 1) * BLK].astype(F32)
 
@@ -183,6 +221,9 @@
     send(S_OFF, LEFT, pack_off.at[0], got_off.at[0])
     send(S_OFF, RIGHT, pack_off.at[1], got_off.at[1])
 
+    for y in (2, 3, 4, 5, 0, 1, 6, 7):
+        hat_load(y).start()
+
     load_src.wait()
     for j in range(NB):
         stage2[j] = raw_src[:, j * BLK:(j + 1) * BLK].astype(F32)
@@ -294,6 +335,7 @@
 
     by_reach(lat, source_columns)
 
+    load_off[2].wait()
     for j in range(1, NB - 1):
         stage_off(j)
 
@@ -319,6 +361,9 @@
     lax.fori_loop(0, ROWS, cur_row, 0)
     pack_cur[0] = pack_tiles([cur_staged(y, 0) for y in range(ROWS)], 0).astype(BF)
     pack_cur[1] = pack_tiles([cur_staged(y, NB - 1) for y in range(ROWS)], 1).astype(BF)
+
+    send(S_CURM, LEFT, pack_cur.at[0], got_cur.at[0])
+    send(S_CURM, RIGHT, pack_cur.at[1], got_cur.at[1])
 
     for load in load_weights:
         load.wait()
@@ -348,16 +393,14 @@
         return spread(jnp.dot(weight, x, preferred_element_type=F32))
 
     def row_out(kind, buf, m, n):
-        send(kind, UP, buf.at[m + n], buf.at[ROWS + m + n])
-        send(kind, DOWN, buf.at[ROWS + m - 1 - n], buf.at[m - 1 - n])
+        rows_send(kind, buf.at[m + n], buf.at[ROWS + m + n],
+                  buf.at[ROWS + m - 1 - n], buf.at[m - 1 - n])
 
     def row_in(kind, buf, m, n):
-        wait_recv(kind, UP, buf.at[m - 1 - n])
-        wait_recv(kind, DOWN, buf.at[ROWS + m + n])
+        rows_recv(kind, buf.at[m - 1 - n], buf.at[ROWS + m + n])
 
     def row_sent(kind, buf, m, n):
-        wait_send(kind, UP, buf.at[m + n])
-        wait_send(kind, DOWN, buf.at[ROWS + m - 1 - n])
+        rows_sent(kind, buf.at[m + n], buf.at[ROWS + m - 1 - n])
 
     def rows_loop(lo, hi, fn):
         lax.fori_loop(lo, hi, fn, 0, unroll=True)
@@ -370,14 +413,18 @@
 
     wait_recv(S_OFF, RIGHT, got_off.at[0])
     wait_recv(S_OFF, LEFT, got_off.at[1])
-    for y in range(ROWS):
+    def v0_margin(y):
         v0[y + 1, 0:CIN, COLS:WIDE] = unpack(
             got_off[0, 0:CIN, :].astype(F32), got_off[1, 0:CIN, :].astype(F32), y).astype(BF)
+
+    v0_margin(0)
+    v0_margin(ROWS - 1)
     part_out[0] = spread(jnp.dot(w1[:, 2 * CPAD:], v0[1], preferred_element_type=F32)).astype(BF)
     part_out[1] = spread(jnp.dot(w1[:, :CPAD], v0[ROWS], preferred_element_type=F32)).astype(BF)
-    send(S_PART, UP, part_out.at[0], part_in.at[1])
-    send(S_PART, DOWN, part_out.at[1], part_in.at[0])
+    rows_send(S_PART, part_out.at[0], part_in.at[1], part_out.at[1], part_in.at[0])
     source_rows()
+    for y in range(1, ROWS - 1):
+        v0_margin(y)
 
     def h1_row(y, _):
         h1[y + 2] = leaky(conv_row(v0, y, w1[...])).astype(BF)
@@ -414,18 +461,11 @@
     rows_loop(2, ROWS - 2, lambda y, _: sample_row(y, near, lat * ROWS, ROWS))
     win[2:2 + ROWS] = near[...]
 
-    wait_recv(S_PART, UP, part_in.at[0])
-    wait_recv(S_PART, DOWN, part_in.at[1])
+    rows_recv(S_PART, part_in.at[0], part_in.at[1])
     h1[2] = leaky(part_own[0] + part_in[0].astype(F32)).astype(BF)
     h1[ROWS + 1] = leaky(part_own[1] + part_in[1].astype(F32)).astype(BF)
 
     row_out(S_H1, h1, 2, 0)
-
-    for side, dirs in ((0, (LEFT, UL, DL)), (1, (RIGHT, UR, DR))):
-        for d in dirs:
-            send(S_CURM, d, pack_cur.at[side], got_cur.at[OPP[d]])
-    send(S_CUR, UP, joined.at[1, 0:64, 0:COLS], joined.at[ROWS + 1, 0:64, 0:COLS])
-    send(S_CUR, DOWN, joined.at[ROWS, 0:64, 0:COLS], joined.at[0, 0:64, 0:COLS])
 
     def in_frame(y):
         g = lat * ROWS + y
@@ -462,37 +502,56 @@
 
     rows_loop(2, ROWS - 2, aligned_row)
 
+    wait_recv(S_CURM, RIGHT, got_cur.at[0])
+    wait_recv(S_CURM, LEFT, got_cur.at[1])
+    for y in range(ROWS):
+        joined[y + 1, 0:64, COLS:WIDE] = unpack(
+            got_cur[0].astype(F32), got_cur[1].astype(F32), y).astype(BF)
     row_in(S_H1_IN, h1, 2, 1)
     row_in(S_H1, h1, 2, 0)
+    rows_send(S_CUR, joined.at[1, 0:64], joined.at[ROWS + 1, 0:64],
+              joined.at[ROWS, 0:64], joined.at[0, 0:64])
     rows_loop(0, 4, ring4(h2_row))
-    rows_loop(0, 4, edge4(aligned_row))
+    aligned_row(0, 0)
+    aligned_row(ROWS - 1, 0)
 
     send(S_AL, UP, joined.at[1, 64:128, 0:COLS], joined.at[ROWS + 1, 64:128, 0:COLS])
     send(S_AL, DOWN, joined.at[ROWS, 64:128, 0:COLS], joined.at[0, 64:128, 0:COLS])
+    aligned_row(1, 0)
+    aligned_row(ROWS - 2, 0)
+    def corner_tile(i):
+        first = joined[i, 64:128, 0:BLK].astype(F32)
+        last = joined[i, 64:128, COLS - BLK:COLS].astype(F32)
+        return squeeze(jnp.where(lane < 64, first, last))
+
+    sq_out[S_ALM, 0] = corner_tile(1)
+    sq_out[S_ALM, 1] = corner_tile(ROWS)
+    for side, d in AL_CORNERS:
+        send(S_ALM, d, sq_out.at[S_ALM, side], got_corner.at[OPP[d]])
     pack_al[0] = pack_tiles(
         [joined[y + 1, 64:128, 0:BLK].astype(F32) for y in range(ROWS)], 0).astype(BF)
     pack_al[1] = pack_tiles(
         [joined[y + 1, 64:128, COLS - BLK:COLS].astype(F32) for y in range(ROWS)], 1).astype(BF)
-    for side, dirs in ((0, (LEFT, UL, DL)), (1, (RIGHT, UR, DR))):
-        for d in dirs:
-            send(S_ALM, d, pack_al.at[side], got_al.at[OPP[d]])
-
-    def margins(kind, got, lo):
-        for d in range(8):
-            if d not in (UP, DOWN):
-                wait_recv(kind, d, got.at[d])
-
-        def put(i, from_right, from_left, y):
-            joined[i, lo:lo + 64, COLS:WIDE] = unpack(
-                got[from_right].astype(F32), got[from_left].astype(F32), y).astype(BF)
-
-        for y in range(ROWS):
-            put(y + 1, RIGHT, LEFT, y)
-        put(0, UR, UL, ROWS - 1)
-        put(ROWS + 1, DR, DL, 0)
-
-    margins(S_CURM, got_cur, 0)
-    margins(S_ALM, got_al, 64)
+    send(S_ALM, LEFT, pack_al.at[0], got_al.at[0])
+    send(S_ALM, RIGHT, pack_al.at[1], got_al.at[1])
+    wait_recv(S_ALM, RIGHT, got_al.at[0])
+    wait_recv(S_ALM, LEFT, got_al.at[1])
+    for y in range(ROWS):
+        joined[y + 1, 64:128, COLS:WIDE] = unpack(
+            got_al[0].astype(F32), got_al[1].astype(F32), y).astype(BF)
+
+    def corners_in():
+        for _, d in AL_CORNERS:
+            wait_recv(S_ALM, d, got_corner.at[d])
+
+        def put(i, from_right, from_left):
+            for k in range(4):
+                a, b = expand(got_corner[from_right], k), expand(got_corner[from_left], k)
+                wide = jnp.where(lane < 8, a, jnp.where(lane >= 120, b, 0.0))
+                joined[i, 64 + 16 * k:80 + 16 * k, COLS:WIDE] = wide.astype(BF)
+
+        pl.when(has_up)(lambda: put(0, UR, UL))
+        pl.when(has_down)(lambda: put(ROWS + 1, DR, DL))
 
     def t0_row(y, _):
         t0[y + 2] = leaky(conv_row(joined, y, wg[...])).astype(BF)
@@ -523,8 +582,8 @@
     t0_row(ROWS - 2, 0)
     row_out(S_T0_IN, t0, 2, 1)
     rows_loop(2, ROWS - 2, t0_row)
-    wait_recv(S_CUR, UP, joined.at[0, 0:64, 0:COLS])
-    wait_recv(S_CUR, DOWN, joined.at[ROWS + 1, 0:64, 0:COLS])
+    rows_recv(S_CUR, joined.at[0, 0:64], joined.at[ROWS + 1, 0:64])
+    corners_in()
     wait_recv(S_AL, UP, joined.at[0, 64:128, 0:COLS])
     wait_recv(S_AL, DOWN, joined.at[ROWS + 1, 64:128, 0:COLS])
     t0_row(0, 0)
@@ -563,14 +622,14 @@
     by_reach(lat, source_columns_sent)
     source_rows_sent()
     each_relay(relay_sent)
-    wait_send(S_PART, UP, part_out.at[0])
-    wait_send(S_PART, DOWN, part_out.at[1])
-    for side, dirs in ((0, (LEFT, UL, DL)), (1, (RIGHT, UR, DR))):
-        for d in dirs:
-            wait_send(S_CURM, d, pack_cur.at[side])
-            wait_send(S_ALM, d, pack_al.at[side])
-    wait_send(S_CUR, UP, joined.at[1, 0:64, 0:COLS])
-    wait_send(S_CUR, DOWN, joined.at[ROWS, 0:64, 0:COLS])
+    rows_sent(S_PART, part_out.at[0], part_out.at[1])
+    for side, d in AL_CORNERS:
+        wait_send(S_ALM, d, sq_out.at[S_ALM, side])
+    wait_send(S_ALM, LEFT, pack_al.at[0])
+    wait_send(S_ALM, RIGHT, pack_al.at[1])
+    wait_send(S_CURM, LEFT, pack_cur.at[0])
+    wait_send(S_CURM, RIGHT, pack_cur.at[1])
+    rows_sent(S_CUR, joined.at[1, 0:64], joined.at[ROWS, 0:64])
     wait_send(S_AL, UP, joined.at[1, 64:128, 0:COLS])
     wait_send(S_AL, DOWN, joined.at[ROWS, 64:128, 0:COLS])
     for kind, buf in ((S_H1, h1), (S_T0, t0), (S_T1, t1)):
@@ -615,14 +674,15 @@
             V((192, 3 * CPAD), BF), V((192, 192), BF), V((144, 576), BF), V((64, 576), BF),
             V((192, 384), BF), V((4, 192, 192), BF),
             V((2, 208, BLK), BF), V((2, 208, BLK), BF),
-            V((2, 64, BLK), BF), V((8, 64, BLK), BF),
-            V((2, 64, BLK), BF), V((8, 64, BLK), BF),
+            V((2, 64, BLK), BF), V((2, 64, BLK), BF),
+            V((2, 64, BLK), BF), V((2, 64, BLK), BF), V((8, 16, BLK), BF),
             V((2, 64, WIDE), BF), V((2, 64, WIDE), BF), V((2, 64, WIDE), F32),
-            pltpu.SemaphoreType.DMA((11,)),
+            V((KINDS, 2, 16, BLK), BF), V((KINDS, 2, 16, BLK), BF),
+            pltpu.SemaphoreType.DMA((13,)),
             pltpu.SemaphoreType.DMA((ROWS,)),
             pltpu.SemaphoreType.DMA((ROWS,)),
-            pltpu.SemaphoreType.DMA((15, 8)),
-            pltpu.SemaphoreType.DMA((15, 8)),
+            pltpu.SemaphoreType.DMA((2 * KINDS, 8)),
+            pltpu.SemaphoreType.DMA((2 * KINDS, 8)),
         ],
         compiler_params=pltpu.CompilerParams(
             collective_id=0, has_side_effects=True, vmem_limit_bytes=60 * 2**20),

time: 65.5 us -> 61.4 us (0.937)
  the two profiles are of different devices: /device:TPU:4 before, /device:TPU:2 now
where the time goes in v4:
time: 61.4 us; the launch traced here: 61.3 us
  Pallas kernels  59.1 us (96%)
  local copies, waits for them, and re-layouts  2.13 us (3%)
    pallas_call x1, Pallas kernels, shards(): pl.pallas_call(functools.partial(kernel, n_lon, n_lat), out_shape=jax.Sha...  59.1 us
    transpose x1, local copies, waits for them, and re-layouts, shards(): return out.transpose(1, 0, 2)  2.13 us

profile of v4, /device:TPU:2, one launch (start us, length us, event | category | flops | bytes accessed | tf_op | source)
XLA Modules:
  0.0 61.3 jit_solution(3451620010284435074)
XLA Ops:
  0.0 59.1 %shard_map.118 = bf16[8,64,512]{2,1,0:T(8,128)(2,1)} custom-call(bf16[1568,512]{1,0:T(8,128)(2,1)} %bitcast.11, bf16[512,512]{1,0:T(8,128)(2,1)} %bitcast.13, bf16[512,512]{1,0:T(8,128)(2,1)} %bitcast.14, bf16[9,64,196]{2,1,0:T(8,128)(2,1)} %w1_hbm.1, bf16[9,64,64]{2,1,0:T(8,128)(2,1)} %w2_hbm.1, bf16[9,64,144]{2,1,0:T(8,128)(2,1)} %bitcast.15, ...), custom_call_target="tpu_custom_call" | custom-call | tf_op jit(solution)/shard_map/pallas_call | solution.py:648
  59.2 2.1 %copy.13 = bf16[64,8,512]{2,1,0:T(8,128)(2,1)} copy(bf16[64,8,512]{2,0,1:T(8,128)(2,1)} %bitcast.10) | data formatting | bytes 1048576 | tf_op jit(solution)/shard_map/transpose | solution.py:698

commit v5 on v4

--- a/solution.py
+++ b/solution.py
@@ -175,9 +175,9 @@
     def expand(small, k):
         return pltpu.roll(small.astype(F32), 120 - 16 * k, 1)
 
-    def put_margin(row, small):
+    def put_margin(row, small, there):
         for k in range(4):
-            wide = jnp.where((lane < 8) | (lane >= 120), expand(small, k), 0.0)
+            wide = jnp.where(((lane < 8) | (lane >= 120)) & there, expand(small, k), 0.0)
             row[16 * k:16 * k + 16, COLS:WIDE] = wide.astype(BF)
 
     def rows_send(kind, up_row, up_dst, down_row, down_dst):
@@ -193,8 +193,8 @@
         wait_recv(kind + KINDS, DOWN, sq_in.at[kind, 1])
         wait_recv(kind, UP, up_dst.at[:, 0:COLS])
         wait_recv(kind, DOWN, down_dst.at[:, 0:COLS])
-        pl.when(has_up)(lambda: put_margin(up_dst, sq_in[kind, 0]))
-        pl.when(has_down)(lambda: put_margin(down_dst, sq_in[kind, 1]))
+        put_margin(up_dst, sq_in[kind, 0], has_up)
+        put_margin(down_dst, sq_in[kind, 1], has_down)
 
     def rows_sent(kind, up_row, down_row):
         wait_send(kind, UP, up_row.at[:, 0:COLS])
@@ -334,6 +334,7 @@
         each_relay(relay_in)
 
     by_reach(lat, source_columns)
+    source_rows()
 
     load_off[2].wait()
     for j in range(1, NB - 1):
@@ -422,7 +423,6 @@
     part_out[0] = spread(jnp.dot(w1[:, 2 * CPAD:], v0[1], preferred_element_type=F32)).astype(BF)
     part_out[1] = spread(jnp.dot(w1[:, :CPAD], v0[ROWS], preferred_element_type=F32)).astype(BF)
     rows_send(S_PART, part_out.at[0], part_in.at[1], part_out.at[1], part_in.at[0])
-    source_rows()
     for y in range(1, ROWS - 1):
         v0_margin(y)
 
@@ -460,6 +460,7 @@
         hat_load(y).wait()
     rows_loop(2, ROWS - 2, lambda y, _: sample_row(y, near, lat * ROWS, ROWS))
     win[2:2 + ROWS] = near[...]
+    source_rows_in()
 
     rows_recv(S_PART, part_in.at[0], part_in.at[1])
     h1[2] = leaky(part_own[0] + part_in[0].astype(F32)).astype(BF)
@@ -481,7 +482,6 @@
 
     rows_loop(1, ROWS - 1, h2_row)
 
-    source_rows_in()
     source_corners_in()
     for y in (0, 1, ROWS - 2, ROWS - 1):
         hat_load(y).wait()

time: 61.4 us -> 59.4 us (0.967)
  the two profiles are of different devices: /device:TPU:2 before, /device:TPU:4 now
where the time goes in v5:
time: 59.4 us; the launch traced here: 58.8 us
  Pallas kernels  56.7 us (95%)
  local copies, waits for them, and re-layouts  2.13 us (4%)
    pallas_call x1, Pallas kernels, shards(): pl.pallas_call(functools.partial(kernel, n_lon, n_lat), out_shape=jax.Sha...  56.7 us
    transpose x1, local copies, waits for them, and re-layouts, shards(): return out.transpose(1, 0, 2)  2.13 us

profile of v5, /device:TPU:4, one launch (start us, length us, event | category | flops | bytes accessed | tf_op | source)
XLA Modules:
  0.0 58.8 jit_solution(13956518881610328519)
XLA Ops:
  0.0 56.7 %shard_map.118 = bf16[8,64,512]{2,1,0:T(8,128)(2,1)} custom-call(bf16[1568,512]{1,0:T(8,128)(2,1)} %bitcast.11, bf16[512,512]{1,0:T(8,128)(2,1)} %bitcast.13, bf16[512,512]{1,0:T(8,128)(2,1)} %bitcast.14, bf16[9,64,196]{2,1,0:T(8,128)(2,1)} %w1_hbm.1, bf16[9,64,64]{2,1,0:T(8,128)(2,1)} %w2_hbm.1, bf16[9,64,144]{2,1,0:T(8,128)(2,1)} %bitcast.15, ...), custom_call_target="tpu_custom_call" | custom-call | tf_op jit(solution)/shard_map/pallas_call | solution.py:648
  56.7 2.1 %copy.13 = bf16[64,8,512]{2,1,0:T(8,128)(2,1)} copy(bf16[64,8,512]{2,0,1:T(8,128)(2,1)} %bitcast.10) | data formatting | bytes 1048576 | tf_op jit(solution)/shard_map/transpose | solution.py:698

commit v6 on v5

--- a/solution.py
+++ b/solution.py
@@ -488,6 +488,7 @@
     rows_loop(0, 4, edge4(lambda y, _: sample_row(y, win, lat * ROWS - 2, WIN_ROWS)))
 
     def aligned_row(y, _):
+        half = y % 2
         x = h2[pl.ds(y, 3)].reshape(576, WIDE)[:, 0:COLS]
         logits = jnp.dot(wm[...], x, preferred_element_type=F32)
         mod = 1.0 / (1.0 + jnp.exp(-logits))
@@ -495,22 +496,26 @@
             m = mod[t * 16:(t + 1) * 16]
             for k in range(4):
                 lo = t * 64 + k * 16
-                modulated[lo:lo + 16, :] = (m * sampled[y, lo:lo + 16, :]).astype(BF)
+                modulated[half, lo:lo + 16, :] = (m * sampled[y, lo:lo + 16, :]).astype(BF)
         joined[y + 1, 64:128, 0:COLS] = jnp.dot(
-            wd[...], modulated[...], preferred_element_type=F32).astype(BF)
+            wd[...], modulated[half], preferred_element_type=F32).astype(BF)
         return 0
 
     rows_loop(2, ROWS - 2, aligned_row)
 
     wait_recv(S_CURM, RIGHT, got_cur.at[0])
     wait_recv(S_CURM, LEFT, got_cur.at[1])
-    for y in range(ROWS):
+
+    def cur_margin(y):
         joined[y + 1, 0:64, COLS:WIDE] = unpack(
             got_cur[0].astype(F32), got_cur[1].astype(F32), y).astype(BF)
+
+    cur_margin(0)
+    cur_margin(ROWS - 1)
+    rows_send(S_CUR, joined.at[1, 0:64], joined.at[ROWS + 1, 0:64],
+              joined.at[ROWS, 0:64], joined.at[0, 0:64])
     row_in(S_H1_IN, h1, 2, 1)
     row_in(S_H1, h1, 2, 0)
-    rows_send(S_CUR, joined.at[1, 0:64], joined.at[ROWS + 1, 0:64],
-              joined.at[ROWS, 0:64], joined.at[0, 0:64])
     rows_loop(0, 4, ring4(h2_row))
     aligned_row(0, 0)
     aligned_row(ROWS - 1, 0)
@@ -534,6 +539,8 @@
         [joined[y + 1, 64:128, COLS - BLK:COLS].astype(F32) for y in range(ROWS)], 1).astype(BF)
     send(S_ALM, LEFT, pack_al.at[0], got_al.at[0])
     send(S_ALM, RIGHT, pack_al.at[1], got_al.at[1])
+    for y in range(1, ROWS - 1):
+        cur_margin(y)
     wait_recv(S_ALM, RIGHT, got_al.at[0])
     wait_recv(S_ALM, LEFT, got_al.at[1])
     for y in range(ROWS):
@@ -662,7 +669,7 @@
             V((ROWS, WIN_COLS, 64, BLK), BF),
             V((WIN_ROWS, WIN_COLS, 64, BLK), BF),
             V((ROWS, TAPS * 64, COLS), F32),
-            V((TAPS * 64, COLS), BF),
+            V((2, TAPS * 64, COLS), BF),
             V((ROWS + 2, CPAD, WIDE), BF),
             V((ROWS + 4, 64, WIDE), BF),
             V((ROWS + 2, 192, WIDE), BF),

time: 59.4 us -> 59 us (level)
  Pallas kernels: 56.7 us -> 55.9 us
    pallas_call x1, Pallas kernels: 56.7 us -> 55.9 us  [shards(): pl.pallas_call(functools.partial(kernel, n_lon, n_lat), out_shape=jax.Sha...]
where the time goes in v6:
time: 59 us; the launch traced here: 58.1 us
  Pallas kernels  55.9 us (95%)
  local copies, waits for them, and re-layouts  2.13 us (4%)
    pallas_call x1, Pallas kernels, shards(): pl.pallas_call(functools.partial(kernel, n_lon, n_lat), out_shape=jax.Sha...  55.9 us
    transpose x1, local copies, waits for them, and re-layouts, shards(): return out.transpose(1, 0, 2)  2.13 us

profile of v6, /device:TPU:4, one launch (start us, length us, event | category | flops | bytes accessed | tf_op | source)
XLA Modules:
  0.0 58.1 jit_solution(13861972676083740813)
XLA Ops:
  0.0 55.9 %shard_map.118 = bf16[8,64,512]{2,1,0:T(8,128)(2,1)} custom-call(bf16[1568,512]{1,0:T(8,128)(2,1)} %bitcast.11, bf16[512,512]{1,0:T(8,128)(2,1)} %bitcast.13, bf16[512,512]{1,0:T(8,128)(2,1)} %bitcast.14, bf16[9,64,196]{2,1,0:T(8,128)(2,1)} %w1_hbm.1, bf16[9,64,64]{2,1,0:T(8,128)(2,1)} %w2_hbm.1, bf16[9,64,144]{2,1,0:T(8,128)(2,1)} %bitcast.15, ...), custom_call_target="tpu_custom_call" | custom-call | tf_op jit(solution)/shard_map/pallas_call | solution.py:655
  55.9 2.1 %copy.13 = bf16[64,8,512]{2,1,0:T(8,128)(2,1)} copy(bf16[64,8,512]{2,0,1:T(8,128)(2,1)} %bitcast.10) | data formatting | bytes 1048576 | tf_op jit(solution)/shard_map/transpose | solution.py:705
